TPU v7x, 32 devices: a whole 2x2x4 slice. The times are simulated.
32 devices in a mesh: segment: 2 (over core), seq: 16 (over z, y, x).
Axes of the slice: x: 2, y: 2, z: 4, core: 2. Of those that a mesh axis runs over, the one named last changes fastest.
Arguments:
- activations: bfloat16 [2, 4096, 768], P('segment', 'seq'), may hold values from -6 to 6
- short_filters: bfloat16 [2, 128, 768], replicated, may hold values from -0.5 to 0.5
- long_filters: float32 [2, 4096, 768], P('segment', 'seq'), may hold values from -4 to 4
- skip_gain: float32 [2, 768], replicated, may hold values from -1 to 1
Outputs:
- sections: bfloat16 [2, 4096, 768], P('segment', 'seq')
All inputs are finite; a program needn't handle non-finite values.
Results may differ from a plain program's by a relative error of at most 0.012.
Values may be sent and summed in bfloat16 or wider, within the bound.
No kernel may reach another device: no remote copies, remote signals or barrier semaphores. Data moves between devices by JAX's collectives and lax.ppermute only.
A program may use at most 64 MiB of HBM per device.

v0:
```python
import functools
import math

import jax
import jax.numpy as jnp
import numpy as np
from jax import lax
from jax.experimental import pallas as pl
from jax.experimental.pallas import tpu as pltpu
from jax.sharding import PartitionSpec as P

BOTH = ("segment", "seq")
LANES = 8
MIB = 1024 * 1024


def spread_order(devices, seq_devices):
    half = seq_devices // 2
    along = [place // 2 + place % 2 * half for place in range(2 * half)]
    along += range(2 * half, seq_devices)
    return tuple(
        start + q for start in range(0, devices, seq_devices) for q in along
    )


def tables(real_rows, cols):
    grid_rows = 2 * real_rows + 1
    length = grid_rows * cols
    freqs = real_rows + 1
    k = np.arange(freqs)
    rows = 2.0 * math.pi * ((k[:, None] * np.arange(real_rows)[None, :]) % grid_rows) / grid_rows
    first = np.stack([np.cos(rows), -np.sin(rows)]).reshape(2 * freqs, real_rows)
    row_part = np.kron(first, np.eye(LANES))
    b = np.arange(cols)
    angle = 2.0 * math.pi * (k[:, None] * b[None, :]) / length
    turn = np.concatenate([np.cos(angle), np.sin(angle)], axis=1)
    turn = np.pad(turn, ((0, -freqs % LANES), (0, 0)))
    grid = 2.0 * math.pi * ((b[:, None] * b[None, :]) % cols) / cols
    c, s = np.cos(grid), np.sin(grid)
    parts = [np.block([[c, -s], [s, c]]), row_part]
    lanes = max(part.shape[1] for part in parts)
    stacked = np.concatenate([np.pad(p, ((0, 0), (0, lanes - p.shape[1]))) for p in parts])
    return jnp.asarray(stacked, jnp.bfloat16), jnp.asarray(turn, jnp.float32)


def dot(a, b):
    return jnp.dot(a, b, preferred_element_type=jnp.float32)


def dot_rows(a, b):
    return lax.dot_general(a, b, (((1,), (1,)), ((), ())), preferred_element_type=jnp.float32)


def repeated(rows, count):
    return jnp.concatenate(
        [jnp.broadcast_to(rows[k : k + 1], (LANES, rows.shape[1])) for k in range(count)], axis=0
    )


def identity(size):
    down = lax.broadcasted_iota(jnp.int32, (size, size), 0)
    across = lax.broadcasted_iota(jnp.int32, (size, size), 1)
    return jnp.where(down == across, 1.0, 0.0).astype(jnp.bfloat16)


def send_kernel(
    width,
    owned,
    order,
    place_ref,
    act_ref,
    filt_ref,
    taps_ref,
    gain_ref,
    out_ref,
    own_ref,
    act_held,
    filt_held,
    taps_held,
    gain_held,
    in_sem,
    own_sem,
):
    sections, length, channels = taps_ref.shape
    mine_first = (
        pltpu.make_async_copy(taps_ref, taps_held, own_sem.at[0]),
        pltpu.make_async_copy(gain_ref, gain_held, own_sem.at[1]),
    )
    for copy in mine_first:
        copy.start()
    arriving = (
        pltpu.make_async_copy(act_ref.at[0], act_held, in_sem.at[0]),
        pltpu.make_async_copy(filt_ref.at[0], filt_held, in_sem.at[1]),
    )
    for copy in arriving:
        copy.start()
    eye = identity(128)
    mine = lax.broadcasted_iota(jnp.int32, (width, channels), 0)
    them = lax.broadcasted_iota(jnp.int32, (width, channels), 1)
    place = jnp.int32(0)
    for position, rank in enumerate(order):
        place = place + jnp.where(place_ref[0] == rank, position, 0)
    pick = jnp.where((them == mine + place * owned) & (mine < owned), 1.0, 0.0)
    for copy in mine_first:
        copy.wait()
    for s in range(sections):
        gain = jnp.sum(pick * gain_held[s : s + 1, :], axis=1, keepdims=True)
        own_ref[s * width : (s + 1) * width, :length] = dot_rows(pick.astype(jnp.bfloat16), taps_held[s])
        own_ref[s * width : (s + 1) * width, length:] = jnp.broadcast_to(gain, (width, 128))
    both = []
    for copy, held in zip(arriving, (act_held, filt_held)):
        copy.wait()
        turned = [
            dot_rows(eye, held[:, start : start + 128].astype(jnp.bfloat16))
            for start in range(0, held.shape[1], 128)
        ]
        both.append(jnp.concatenate(turned, axis=0))
    for d in range(len(order)):
        part = slice(d * width, (d + 1) * width)
        piece = jnp.concatenate([array[part] for array in both], axis=0).astype(jnp.bfloat16)
        out_ref[2 * d * width : 2 * (d + 1) * width] = piece


def final_kernel(in_ref, out_ref):
    channels, tokens = in_ref.shape
    step = math.gcd(channels, 256)
    eye = identity(tokens)
    for start in range(0, channels, step):
        part = slice(start, start + step)
        out_ref[0, :, part] = dot_rows(eye, in_ref[part]).astype(jnp.bfloat16)


def main_kernel(width, sections, order, in_ref, own_ref, turn_ref, table_ref, out_ref):
    total, cols = in_ref.shape
    rows = total // (2 * width * sections)
    groups = width // LANES
    high = (rows + 1) * LANES
    span = groups * high
    bf = jnp.bfloat16
    copies = rows + 1
    length = own_ref.shape[1] - 128
    scale = 1.0 / math.sqrt(rows * cols)
    whole = (2 * rows + 1) * cols
    turn = repeated(turn_ref[...], copies)
    cosine, sine = turn[:, :cols], turn[:, cols:]
    all_cos = jnp.concatenate([cosine] * groups, axis=0)
    all_sin = jnp.concatenate([sine] * groups, axis=0)
    forward_cols = table_ref[: 2 * cols, : 2 * cols]
    level, minus = table_ref[:cols, :cols], table_ref[:cols, cols : 2 * cols]
    plus = table_ref[cols : 2 * cols, :cols]
    back_cols = jnp.concatenate(
        [jnp.concatenate([level, plus], axis=1), jnp.concatenate([minus, level], axis=1)], axis=0
    )
    forward_rows = table_ref[2 * cols : 2 * cols + 2 * high, : rows * LANES]
    wide_rows = forward_rows.astype(jnp.float32)
    some_rows = jnp.concatenate([wide_rows[LANES:high], wide_rows[high + LANES :]], axis=0)
    back_rows = dot_rows(identity(rows * LANES), some_rows.astype(bf)).astype(bf)

    def chunk(s):
        starts = [order.index(s * rows + a) * 2 * width for a in range(rows)]
        part = jnp.concatenate([in_ref[at : at + 2 * width] for at in starts], axis=0)
        return part.astype(jnp.float32).reshape(rows, 2 * width, cols)

    def forward(grids):
        turned = []
        for grid in grids:
            for g in range(groups):
                block = grid[:, g * LANES : (g + 1) * LANES].reshape(rows * LANES, cols).astype(bf)
                spread = dot(forward_rows, block)
                real, imag = spread[:high], spread[high:]
                turned.append(
                    jnp.concatenate(
                        [real * cosine + imag * sine, imag * cosine - real * sine], axis=1
                    )
                )
        return dot(jnp.concatenate(turned, axis=0).astype(bf), forward_cols)

    def times(left, right):
        lr, li = left[:, :cols], left[:, cols:]
        rr, ri = right
        return jnp.concatenate([lr * rr - li * ri, lr * ri + li * rr], axis=1).astype(bf)

    def back(product):
        flat = dot(product, back_cols)
        real, imag = flat[:, :cols], flat[:, cols:]
        turned_real = real * all_cos - imag * all_sin
        turned_imag = real * all_sin + imag * all_cos
        pieces = []
        for g in range(groups):
            start = g * high
            part = slice(start + LANES, start + high)
            both = jnp.concatenate([turned_real[part], turned_imag[part]], axis=0).astype(bf)
            piece = dot(back_rows, both).reshape(rows, LANES, cols)
            pieces.append(piece + turned_real[start : start + LANES][None])
        return jnp.concatenate(pieces, axis=1)

    def short_specs():
        turned = []
        for s in range(sections):
            for g in range(groups):
                start = s * width + g * LANES
                taps = jnp.concatenate([own_ref[start : start + LANES, :length]] * copies, axis=0)
                turned.append(
                    jnp.concatenate([taps * short_cos, taps * short_sin], axis=1)
                )
        columns = jnp.concatenate([table_ref[:length, : 2 * cols], table_ref[cols : cols + length, : 2 * cols]])
        return dot(jnp.concatenate(turned, axis=0).astype(bf), columns)

    row = lax.broadcasted_iota(jnp.int32, (high, 1), 0)
    weight = jnp.where(row < LANES, scale / whole, 2.0 * scale / whole)
    short_cos, short_sin = cosine[:, :length] * weight, -(sine[:, :length] * weight)
    shorts = short_specs()

    def combine(s, spec):
        gains = own_ref[s * width : (s + 1) * width, length:] * (1.0 / scale)
        gains = jnp.concatenate([gains] * (cols // 128), axis=1)
        shift = jnp.concatenate(
            [gains[g * LANES : (g + 1) * LANES] for g in range(groups) for _ in range(copies)], axis=0
        )
        short = shorts[s * span : (s + 1) * span]
        lr, li = spec[:, :cols] + shift, spec[:, cols:]
        rr, ri = short[:, :cols], short[:, cols:]
        return lr * rr - li * ri, lr * ri + li * rr

    chunks = [chunk(s) for s in range(sections)]
    specs = forward([chunks[0][:, :width]] + [part[:, width:] for part in chunks])
    signal_spec = specs[:span]
    results = []
    for s in range(sections):
        mixed = combine(s, specs[(s + 1) * span : (s + 2) * span])
        result = back(times(signal_spec, mixed))
        results.append(result)
        if s + 1 < sections:
            rounded = result.astype(bf).astype(jnp.float32)
            signal_spec = forward([rounded * chunks[s + 1][:, :width]])
    for at in range(0, len(order), 2):
        pair = [results[rank // rows][rank % rows] for rank in order[at : at + 2]]
        out_ref[at * width : (at + 2) * width] = jnp.concatenate(pair, axis=0).astype(bf)


def body(activations, short_filters, long_filters, skip_gain):
    sections = short_filters.shape[0]
    tokens, channels = activations.shape[1:]
    devices = lax.axis_size(BOTH)
    seq_devices = lax.axis_size("seq")
    owned = channels // devices
    width = -(-owned // LANES) * LANES
    cols = tokens
    laid = devices * width
    order = spread_order(devices, seq_devices)

    def widen(array):
        split = array.reshape(array.shape[:2] + (devices, owned))
        split = jnp.pad(split, ((0, 0), (0, 0), (0, 0), (0, width - owned)))
        return split.reshape(array.shape[:2] + (laid,))

    def exchanged(array, height):
        chunks = array.reshape(devices, height, cols)
        moved = lax.all_to_all(
            chunks, BOTH, split_axis=0, concat_axis=0, tiled=True, axis_index_groups=[list(order)]
        )
        return moved.reshape(devices * height, cols)

    def grant(size):
        return pltpu.CompilerParams(vmem_limit_bytes=int(size))

    acts, filters = activations, long_filters
    if width != owned:
        acts, filters = widen(acts), widen(filters)
    table, turn = tables(seq_devices, cols)
    vmem = pl.BlockSpec(memory_space=pltpu.VMEM)
    hbm = pl.BlockSpec(memory_space=pltpu.HBM)
    area = laid * cols
    span = (seq_devices + 1) * width
    taps = short_filters.shape[1]
    place = lax.axis_index(BOTH).astype(jnp.int32).reshape(1)
    inputs = (acts, filters, short_filters, skip_gain)
    outgoing, own = pl.pallas_call(
        functools.partial(send_kernel, width, owned, order),
        out_shape=(
            jax.ShapeDtypeStruct((2 * laid, cols), jnp.bfloat16),
            jax.ShapeDtypeStruct((sections * width, taps + 128), jnp.float32),
        ),
        in_specs=[pl.BlockSpec(memory_space=pltpu.SMEM)] + [hbm] * 4,
        out_specs=(vmem, vmem),
        scratch_shapes=[
            pltpu.VMEM((cols, laid), jnp.bfloat16),
            pltpu.VMEM((cols, laid), jnp.float32),
            pltpu.VMEM(short_filters.shape, jnp.bfloat16),
            pltpu.VMEM(skip_gain.shape, jnp.float32),
            pltpu.SemaphoreType.DMA((2,)),
            pltpu.SemaphoreType.DMA((2,)),
        ],
        compiler_params=grant(4 * MIB + 24 * area),
    )(place, *(pltpu.with_memory_space_constraint(array, pltpu.HBM) for array in inputs))
    arrived = exchanged(outgoing, 2 * width)
    results = pl.pallas_call(
        functools.partial(main_kernel, width, sections, order),
        out_shape=jax.ShapeDtypeStruct((laid, cols), jnp.bfloat16),
        in_specs=[vmem] * 4,
        out_specs=vmem,
        compiler_params=grant(2 * MIB + 6 * area + 2 * table.size + 64 * span * cols),
    )(arrived, own, turn, table)
    returned = exchanged(results, width)
    final = pl.pallas_call(
        final_kernel,
        out_shape=jax.ShapeDtypeStruct((1, cols, laid), jnp.bfloat16),
        compiler_params=grant(4 * MIB + 16 * area),
    )(returned)
    if width != owned:
        final = final.reshape(1, cols, devices, width)[..., :owned].reshape(1, cols, channels)
    return final


def solution(mesh):
    return jax.shard_map(
        body,
        mesh=mesh,
        in_specs=(P("segment", "seq", None), P(), P("segment", "seq", None), P()),
        out_specs=P("segment", "seq", None),
        check_vma=False,
    )
```

profile of v0, /device:TPU:0, one launch (start us, length us, event | category | flops | bytes accessed | tf_op | source)
XLA Modules:
  0.0 49.2 jit_solution(3143118000715216583)
XLA Ops:
  0.0 1.8 %shard_map.64 = (bf16[1536,256]{1,0:T(8,128)(2,1)S(1)}, f32[48,256]{1,0:T(8,128)S(1)}) custom-call(s32[1]{0:T(128)} %bitcast.place_ref, bf16[1,256,768]{2,1,0:T(8,128)(2,1)} %act_ref.1, f32[1,256,768]{2,1,0:T(8,128)} %filt_ref.1, bf16[2,128,768]{2,1,0:T(8,128)(2,1)} %taps_ref.1, f32[2,768]{1,0:T(2,128)} %gain_ref.1), custom_call_target="tpu_custom_call" | custom-call | tf_op jit(solution)/shard_map/pallas_call | solution.py:278
  1.9 0.0 copy-start
  1.9 0.0 copy-start.1
  1.9 27.1 %all_to_all.10 = bf16[32,48,256]{2,1,0:T(8,128)(2,1)S(1)} all-to-all(bf16[32,48,256]{2,1,0:T(8,128)(2,1)S(1)} %bitcast.8), channel_id=1, replica_groups={{0,8,1,9,2,10,3,11,4,12,5,13,6,14,7,15,16,24,17,25,18,26,19,27,20,28,21..., dimensions={0} | all-to-all | bytes 1572864 | tf_op jit(solution)/shard_map/all_to_all | solution.py:259
  29.0 0.0 copy-done
  29.0 0.0 copy-done.1
  29.0 3.0 %shard_map.65 = bf16[768,256]{1,0:T(8,128)(2,1)S(1)} custom-call(bf16[1536,256]{1,0:T(8,128)(2,1)S(1)} %bitcast.5, f32[48,256]{1,0:T(8,128)S(1)} %get-tuple-element.8.own_ref, f32[24,512]{1,0:T(8,128)S(1)} %copy-done.1, bf16[784,512]{1,0:T(8,128)(2,1)S(1)} %copy-done), custom_call_target="tpu_custom_call" | custom-call | tf_op jit(solution)/shard_map/pallas_call | solution.py:297
  32.0 16.2 %all_to_all.11 = bf16[32,24,256]{2,1,0:T(8,128)(2,1)S(1)} all-to-all(bf16[32,24,256]{2,1,0:T(8,128)(2,1)S(1)} %bitcast.7), channel_id=1, replica_groups={{0,8,1,9,2,10,3,11,4,12,5,13,6,14,7,15,16,24,17,25,18,26,19,27,20,28,21..., dimensions={0} | all-to-all | bytes 786432 | tf_op jit(solution)/shard_map/all_to_all | solution.py:259
  48.2 1.0 %shard_map.66 = bf16[1,256,768]{2,1,0:T(8,128)(2,1)} custom-call(bf16[768,256]{1,0:T(8,128)(2,1)S(1)} %bitcast.6), custom_call_target="tpu_custom_call" | custom-call | tf_op jit(solution)/shard_map/pallas_call | solution.py:305
Async XLA Ops:
  1.9 27.1 %copy-start = (bf16[784,512]{1,0:T(8,128)(2,1)S(1)}, bf16[784,512]{1,0:T(8,128)(2,1)}, u32[]{:S(2)}) copy-start(bf16[784,512]{1,0:T(8,128)(2,1)} %constant.15.clone.table_ref) | copy-start | bytes 2408452
  1.9 27.1 %copy-start.1 = (f32[24,512]{1,0:T(8,128)S(1)}, f32[24,512]{1,0:T(8,128)}, u32[]{:S(2)}) copy-start(f32[24,512]{1,0:T(8,128)} %constant.16.clone.turn_ref) | copy-start | bytes 147460
where the time goes:
time: 49.5 us; the launch traced here: 49.2 us
  blocking collectives  43.3 us (87%)
  Pallas kernels  5.9 us (12%)
    all_to_all x2, blocking collectives, exchanged(): lax.all_to_all(chunks, BOTH, split_axis=0, concat_axis=0, tiled=True, axi...  43.3 us
    pallas_call x1, Pallas kernels, body(): pl.pallas_call(functools.partial(main_kernel, width, sections, order), ou...  3.01 us
    pallas_call x1, Pallas kernels, body(): pl.pallas_call(functools.partial(send_kernel, width, owned, order), out_s...  1.84 us
    pallas_call x1, Pallas kernels, body(): pl.pallas_call(final_kernel, out_shape=jax.ShapeDtypeStruct((1, cols, lai...  1.05 us

commit v1 on v0

--- a/solution.py
+++ b/solution.py
@@ -23,12 +23,13 @@
     )
 
 
-def tables(real_rows, cols):
+def tables(real_rows, cols, split):
     grid_rows = 2 * real_rows + 1
     length = grid_rows * cols
     freqs = real_rows + 1
     k = np.arange(freqs)
-    rows = 2.0 * math.pi * ((k[:, None] * np.arange(real_rows)[None, :]) % grid_rows) / grid_rows
+    place = np.arange(real_rows).reshape(-1, split).T.reshape(-1)
+    rows = 2.0 * math.pi * ((k[:, None] * place[None, :]) % grid_rows) / grid_rows
     first = np.stack([np.cos(rows), -np.sin(rows)]).reshape(2 * freqs, real_rows)
     row_part = np.kron(first, np.eye(LANES))
     b = np.arange(cols)
@@ -130,9 +131,11 @@
         out_ref[0, :, part] = dot_rows(eye, in_ref[part]).astype(jnp.bfloat16)
 
 
-def main_kernel(width, sections, order, in_ref, own_ref, turn_ref, table_ref, out_ref):
-    total, cols = in_ref.shape
-    rows = total // (2 * width * sections)
+def main_kernel(width, sections, split, order, in_ref, own_ref, turn_ref, table_ref, out_ref):
+    total, tokens = in_ref.shape
+    cols = tokens // split
+    seq = total // (2 * width * sections)
+    rows = seq * split
     groups = width // LANES
     high = (rows + 1) * LANES
     span = groups * high
@@ -157,22 +160,25 @@
     back_rows = dot_rows(identity(rows * LANES), some_rows.astype(bf)).astype(bf)
 
     def chunk(s):
-        starts = [order.index(s * rows + a) * 2 * width for a in range(rows)]
+        starts = [order.index(s * seq + q) * 2 * width for q in range(seq)]
         part = jnp.concatenate([in_ref[at : at + 2 * width] for at in starts], axis=0)
-        return part.astype(jnp.float32).reshape(rows, 2 * width, cols)
+        return part.astype(jnp.float32).reshape(seq, 2 * width, tokens)
 
     def forward(grids):
-        turned = []
+        blocks = []
         for grid in grids:
             for g in range(groups):
-                block = grid[:, g * LANES : (g + 1) * LANES].reshape(rows * LANES, cols).astype(bf)
-                spread = dot(forward_rows, block)
-                real, imag = spread[:high], spread[high:]
-                turned.append(
-                    jnp.concatenate(
-                        [real * cosine + imag * sine, imag * cosine - real * sine], axis=1
-                    )
-                )
+                part = grid[:, g * LANES : (g + 1) * LANES]
+                parts = [part[:, :, h * cols : (h + 1) * cols] for h in range(split)]
+                blocks.append(jnp.concatenate(parts, axis=0).reshape(rows * LANES, cols))
+        spread = dot(forward_rows, jnp.concatenate(blocks, axis=1).astype(bf))
+        turned = []
+        for n in range(len(blocks)):
+            lanes = slice(n * cols, (n + 1) * cols)
+            real, imag = spread[:high, lanes], spread[high:, lanes]
+            turned.append(
+                jnp.concatenate([real * cosine + imag * sine, imag * cosine - real * sine], axis=1)
+            )
         return dot(jnp.concatenate(turned, axis=0).astype(bf), forward_cols)
 
     def times(left, right):
@@ -185,13 +191,17 @@
         real, imag = flat[:, :cols], flat[:, cols:]
         turned_real = real * all_cos - imag * all_sin
         turned_imag = real * all_sin + imag * all_cos
+        joined = []
+        for g in range(groups):
+            part = slice(g * high + LANES, (g + 1) * high)
+            joined.append(jnp.concatenate([turned_real[part], turned_imag[part]], axis=0))
+        spread = dot(back_rows, jnp.concatenate(joined, axis=1).astype(bf))
         pieces = []
         for g in range(groups):
-            start = g * high
-            part = slice(start + LANES, start + high)
-            both = jnp.concatenate([turned_real[part], turned_imag[part]], axis=0).astype(bf)
-            piece = dot(back_rows, both).reshape(rows, LANES, cols)
-            pieces.append(piece + turned_real[start : start + LANES][None])
+            piece = spread[:, g * cols : (g + 1) * cols].reshape(rows, LANES, cols)
+            piece = piece + turned_real[g * high : g * high + LANES][None]
+            parts = [piece[h * seq : (h + 1) * seq] for h in range(split)]
+            pieces.append(jnp.concatenate(parts, axis=2))
         return jnp.concatenate(pieces, axis=1)
 
     def short_specs():
@@ -234,7 +244,7 @@
             rounded = result.astype(bf).astype(jnp.float32)
             signal_spec = forward([rounded * chunks[s + 1][:, :width]])
     for at in range(0, len(order), 2):
-        pair = [results[rank // rows][rank % rows] for rank in order[at : at + 2]]
+        pair = [results[rank // seq][rank % seq] for rank in order[at : at + 2]]
         out_ref[at * width : (at + 2) * width] = jnp.concatenate(pair, axis=0).astype(bf)
 
 
@@ -267,7 +277,8 @@
     acts, filters = activations, long_filters
     if width != owned:
         acts, filters = widen(acts), widen(filters)
-    table, turn = tables(seq_devices, cols)
+    split = 2 if seq_devices <= 32 and cols % 256 == 0 else 1
+    table, turn = tables(seq_devices * split, cols // split, split)
     vmem = pl.BlockSpec(memory_space=pltpu.VMEM)
     hbm = pl.BlockSpec(memory_space=pltpu.HBM)
     area = laid * cols
@@ -295,7 +306,7 @@
     )(place, *(pltpu.with_memory_space_constraint(array, pltpu.HBM) for array in inputs))
     arrived = exchanged(outgoing, 2 * width)
     results = pl.pallas_call(
-        functools.partial(main_kernel, width, sections, order),
+        functools.partial(main_kernel, width, sections, split, order),
         out_shape=jax.ShapeDtypeStruct((laid, cols), jnp.bfloat16),
         in_specs=[vmem] * 4,
         out_specs=vmem,

time: 49.5 us -> 49.2 us (level)
  no operation moved by 1% of the time
where the time goes in v1:
time: 49.2 us; the launch traced here: 48.9 us
  blocking collectives  43.3 us (88%)
  Pallas kernels  5.64 us (11%)
    all_to_all x2, blocking collectives, exchanged(): lax.all_to_all(chunks, BOTH, split_axis=0, concat_axis=0, tiled=True, axi...  43.3 us
    pallas_call x1, Pallas kernels, body(): pl.pallas_call(functools.partial(main_kernel, width, sections, split, ord...  2.75 us
    pallas_call x1, Pallas kernels, body(): pl.pallas_call(functools.partial(send_kernel, width, owned, order), out_s...  1.84 us
    pallas_call x1, Pallas kernels, body(): pl.pallas_call(final_kernel, out_shape=jax.ShapeDtypeStruct((1, cols, lai...  1.05 us

profile of v1, /device:TPU:0, one launch (start us, length us, event | category | flops | bytes accessed | tf_op | source)
XLA Modules:
  0.0 48.9 jit_solution(14465609469385811640)
XLA Ops:
  0.0 1.8 %shard_map.64 = (bf16[1536,256]{1,0:T(8,128)(2,1)S(1)}, f32[48,256]{1,0:T(8,128)S(1)}) custom-call(s32[1]{0:T(128)} %bitcast.place_ref, bf16[1,256,768]{2,1,0:T(8,128)(2,1)} %act_ref.1, f32[1,256,768]{2,1,0:T(8,128)} %filt_ref.1, bf16[2,128,768]{2,1,0:T(8,128)(2,1)} %taps_ref.1, f32[2,768]{1,0:T(2,128)} %gain_ref.1), custom_call_target="tpu_custom_call" | custom-call | tf_op jit(solution)/shard_map/pallas_call | solution.py:289
  1.9 0.0 copy-start
  1.9 0.0 copy-start.1
  1.9 27.1 %all_to_all.10 = bf16[32,48,256]{2,1,0:T(8,128)(2,1)S(1)} all-to-all(bf16[32,48,256]{2,1,0:T(8,128)(2,1)S(1)} %bitcast.8), channel_id=1, replica_groups={{0,8,1,9,2,10,3,11,4,12,5,13,6,14,7,15,16,24,17,25,18,26,19,27,20,28,21..., dimensions={0} | all-to-all | bytes 1572864 | tf_op jit(solution)/shard_map/all_to_all | solution.py:269
  29.0 0.0 copy-done
  29.0 0.0 copy-done.1
  29.0 2.7 %shard_map.65 = bf16[768,256]{1,0:T(8,128)(2,1)S(1)} custom-call(bf16[1536,256]{1,0:T(8,128)(2,1)S(1)} %bitcast.5, f32[48,256]{1,0:T(8,128)S(1)} %get-tuple-element.8.own_ref, f32[40,256]{1,0:T(8,128)S(1)} %copy-done.1, bf16[784,256]{1,0:T(8,128)(2,1)S(1)} %copy-done), custom_call_target="tpu_custom_call" | custom-call | tf_op jit(solution)/shard_map/pallas_call | solution.py:308
  31.7 16.2 %all_to_all.11 = bf16[32,24,256]{2,1,0:T(8,128)(2,1)S(1)} all-to-all(bf16[32,24,256]{2,1,0:T(8,128)(2,1)S(1)} %bitcast.7), channel_id=1, replica_groups={{0,8,1,9,2,10,3,11,4,12,5,13,6,14,7,15,16,24,17,25,18,26,19,27,20,28,21..., dimensions={0} | all-to-all | bytes 786432 | tf_op jit(solution)/shard_map/all_to_all | solution.py:269
  47.9 1.0 %shard_map.66 = bf16[1,256,768]{2,1,0:T(8,128)(2,1)} custom-call(bf16[768,256]{1,0:T(8,128)(2,1)S(1)} %bitcast.6), custom_call_target="tpu_custom_call" | custom-call | tf_op jit(solution)/shard_map/pallas_call | solution.py:316
Async XLA Ops:
  1.9 27.1 %copy-start = (bf16[784,256]{1,0:T(8,128)(2,1)S(1)}, bf16[784,256]{1,0:T(8,128)(2,1)}, u32[]{:S(2)}) copy-start(bf16[784,256]{1,0:T(8,128)(2,1)} %constant.15.clone.table_ref) | copy-start | bytes 1204228
  1.9 27.1 %copy-start.1 = (f32[40,256]{1,0:T(8,128)S(1)}, f32[40,256]{1,0:T(8,128)}, u32[]{:S(2)}) copy-start(f32[40,256]{1,0:T(8,128)} %constant.16.clone.turn_ref) | copy-start | bytes 122884

commit v2 on v1

--- a/solution.py
+++ b/solution.py
@@ -89,10 +89,12 @@
     )
     for copy in mine_first:
         copy.start()
-    arriving = (
-        pltpu.make_async_copy(act_ref.at[0], act_held, in_sem.at[0]),
-        pltpu.make_async_copy(filt_ref.at[0], filt_held, in_sem.at[1]),
-    )
+    half = act_ref.shape[1] // 2
+    arriving = [
+        pltpu.make_async_copy(filt_ref.at[0, :half], filt_held.at[:half], in_sem.at[0]),
+        pltpu.make_async_copy(act_ref.at[0], act_held, in_sem.at[1]),
+        pltpu.make_async_copy(filt_ref.at[0, half:], filt_held.at[half:], in_sem.at[2]),
+    ]
     for copy in arriving:
         copy.start()
     eye = identity(128)
@@ -108,14 +110,15 @@
         gain = jnp.sum(pick * gain_held[s : s + 1, :], axis=1, keepdims=True)
         own_ref[s * width : (s + 1) * width, :length] = dot_rows(pick.astype(jnp.bfloat16), taps_held[s])
         own_ref[s * width : (s + 1) * width, length:] = jnp.broadcast_to(gain, (width, 128))
-    both = []
-    for copy, held in zip(arriving, (act_held, filt_held)):
+    turned = []
+    for copy, held in zip(arriving, (filt_held.at[:half], act_held, filt_held.at[half:])):
         copy.wait()
-        turned = [
+        columns = [
             dot_rows(eye, held[:, start : start + 128].astype(jnp.bfloat16))
             for start in range(0, held.shape[1], 128)
         ]
-        both.append(jnp.concatenate(turned, axis=0))
+        turned.append(jnp.concatenate(columns, axis=0))
+    both = (turned[1], jnp.concatenate([turned[0], turned[2]], axis=1))
     for d in range(len(order)):
         part = slice(d * width, (d + 1) * width)
         piece = jnp.concatenate([array[part] for array in both], axis=0).astype(jnp.bfloat16)
@@ -138,7 +141,6 @@
     rows = seq * split
     groups = width // LANES
     high = (rows + 1) * LANES
-    span = groups * high
     bf = jnp.bfloat16
     copies = rows + 1
     length = own_ref.shape[1] - 128
@@ -146,8 +148,6 @@
     whole = (2 * rows + 1) * cols
     turn = repeated(turn_ref[...], copies)
     cosine, sine = turn[:, :cols], turn[:, cols:]
-    all_cos = jnp.concatenate([cosine] * groups, axis=0)
-    all_sin = jnp.concatenate([sine] * groups, axis=0)
     forward_cols = table_ref[: 2 * cols, : 2 * cols]
     level, minus = table_ref[:cols, :cols], table_ref[:cols, cols : 2 * cols]
     plus = table_ref[cols : 2 * cols, :cols]
@@ -166,8 +166,8 @@
 
     def forward(grids):
         blocks = []
-        for grid in grids:
-            for g in range(groups):
+        for g in over:
+            for grid in grids:
                 part = grid[:, g * LANES : (g + 1) * LANES]
                 parts = [part[:, :, h * cols : (h + 1) * cols] for h in range(split)]
                 blocks.append(jnp.concatenate(parts, axis=0).reshape(rows * LANES, cols))
@@ -179,70 +179,69 @@
             turned.append(
                 jnp.concatenate([real * cosine + imag * sine, imag * cosine - real * sine], axis=1)
             )
-        return dot(jnp.concatenate(turned, axis=0).astype(bf), forward_cols)
+        count = len(grids)
+        stacked = [jnp.concatenate(turned[g * count : (g + 1) * count], axis=0) for g in over]
+        return [dot(part.astype(bf), forward_cols) for part in stacked]
 
     def times(left, right):
         lr, li = left[:, :cols], left[:, cols:]
         rr, ri = right
         return jnp.concatenate([lr * rr - li * ri, lr * ri + li * rr], axis=1).astype(bf)
 
-    def back(product):
-        flat = dot(product, back_cols)
-        real, imag = flat[:, :cols], flat[:, cols:]
-        turned_real = real * all_cos - imag * all_sin
-        turned_imag = real * all_sin + imag * all_cos
-        joined = []
-        for g in range(groups):
-            part = slice(g * high + LANES, (g + 1) * high)
-            joined.append(jnp.concatenate([turned_real[part], turned_imag[part]], axis=0))
+    def back(products):
+        joined, firsts = [], []
+        for flat in [dot(product, back_cols) for product in products]:
+            real, imag = flat[:, :cols], flat[:, cols:]
+            turned_real = real * cosine - imag * sine
+            turned_imag = real * sine + imag * cosine
+            firsts.append(turned_real[:LANES][None])
+            joined.append(jnp.concatenate([turned_real[LANES:], turned_imag[LANES:]], axis=0))
         spread = dot(back_rows, jnp.concatenate(joined, axis=1).astype(bf))
         pieces = []
-        for g in range(groups):
-            piece = spread[:, g * cols : (g + 1) * cols].reshape(rows, LANES, cols)
-            piece = piece + turned_real[g * high : g * high + LANES][None]
+        for g in over:
+            piece = spread[:, g * cols : (g + 1) * cols].reshape(rows, LANES, cols) + firsts[g]
             parts = [piece[h * seq : (h + 1) * seq] for h in range(split)]
             pieces.append(jnp.concatenate(parts, axis=2))
         return jnp.concatenate(pieces, axis=1)
 
-    def short_specs():
-        turned = []
-        for s in range(sections):
-            for g in range(groups):
-                start = s * width + g * LANES
-                taps = jnp.concatenate([own_ref[start : start + LANES, :length]] * copies, axis=0)
-                turned.append(
-                    jnp.concatenate([taps * short_cos, taps * short_sin], axis=1)
-                )
-        columns = jnp.concatenate([table_ref[:length, : 2 * cols], table_ref[cols : cols + length, : 2 * cols]])
-        return dot(jnp.concatenate(turned, axis=0).astype(bf), columns)
-
     row = lax.broadcasted_iota(jnp.int32, (high, 1), 0)
     weight = jnp.where(row < LANES, scale / whole, 2.0 * scale / whole)
     short_cos, short_sin = cosine[:, :length] * weight, -(sine[:, :length] * weight)
-    shorts = short_specs()
-
-    def combine(s, spec):
-        gains = own_ref[s * width : (s + 1) * width, length:] * (1.0 / scale)
+    short_cols = jnp.concatenate(
+        [table_ref[:length, : 2 * cols], table_ref[cols : cols + length, : 2 * cols]], axis=0
+    )
+
+    def short_half(s, g):
+        start = s * width + g * LANES
+        taps = jnp.concatenate([own_ref[start : start + LANES, :length]] * copies, axis=0)
+        return jnp.concatenate([taps * short_cos, taps * short_sin], axis=1)
+
+    def combine(s, g, short, spec):
+        start = s * width + g * LANES
+        gains = own_ref[start : start + LANES, length:] * (1.0 / scale)
         gains = jnp.concatenate([gains] * (cols // 128), axis=1)
-        shift = jnp.concatenate(
-            [gains[g * LANES : (g + 1) * LANES] for g in range(groups) for _ in range(copies)], axis=0
-        )
-        short = shorts[s * span : (s + 1) * span]
-        lr, li = spec[:, :cols] + shift, spec[:, cols:]
+        lr, li = spec[:, :cols] + jnp.concatenate([gains] * copies, axis=0), spec[:, cols:]
         rr, ri = short[:, :cols], short[:, cols:]
         return lr * rr - li * ri, lr * ri + li * rr
 
+    over = range(groups)
     chunks = [chunk(s) for s in range(sections)]
     specs = forward([chunks[0][:, :width]] + [part[:, width:] for part in chunks])
-    signal_spec = specs[:span]
+    signals = [spec[:high] for spec in specs]
+    shorts = [
+        dot(jnp.concatenate([short_half(s, g) for s in range(sections)], axis=0).astype(bf), short_cols)
+        for g in over
+    ]
     results = []
     for s in range(sections):
-        mixed = combine(s, specs[(s + 1) * span : (s + 2) * span])
-        result = back(times(signal_spec, mixed))
+        part, after = slice(s * high, (s + 1) * high), slice((s + 1) * high, (s + 2) * high)
+        result = back(
+            [times(signals[g], combine(s, g, shorts[g][part], specs[g][after])) for g in over]
+        )
         results.append(result)
         if s + 1 < sections:
             rounded = result.astype(bf).astype(jnp.float32)
-            signal_spec = forward([rounded * chunks[s + 1][:, :width]])
+            signals = forward([rounded * chunks[s + 1][:, :width]])
     for at in range(0, len(order), 2):
         pair = [results[rank // seq][rank % seq] for rank in order[at : at + 2]]
         out_ref[at * width : (at + 2) * width] = jnp.concatenate(pair, axis=0).astype(bf)
@@ -299,7 +298,7 @@
             pltpu.VMEM((cols, laid), jnp.float32),
             pltpu.VMEM(short_filters.shape, jnp.bfloat16),
             pltpu.VMEM(skip_gain.shape, jnp.float32),
-            pltpu.SemaphoreType.DMA((2,)),
+            pltpu.SemaphoreType.DMA((3,)),
             pltpu.SemaphoreType.DMA((2,)),
         ],
         compiler_params=grant(4 * MIB + 24 * area),

time: 49.2 us -> 49.6 us (level)
  no operation moved by 1% of the time
where the time goes in v2:
time: 49.6 us; the launch traced here: 49.3 us
  blocking collectives  43.3 us (87%)
  Pallas kernels  6.04 us (12%)
    all_to_all x2, blocking collectives, exchanged(): lax.all_to_all(chunks, BOTH, split_axis=0, concat_axis=0, tiled=True, axi...  43.3 us
    pallas_call x1, Pallas kernels, body(): pl.pallas_call(functools.partial(main_kernel, width, sections, split, ord...  2.78 us
    pallas_call x1, Pallas kernels, body(): pl.pallas_call(functools.partial(send_kernel, width, owned, order), out_s...  2.22 us
    pallas_call x1, Pallas kernels, body(): pl.pallas_call(final_kernel, out_shape=jax.ShapeDtypeStruct((1, cols, lai...  1.05 us

profile of v2, /device:TPU:0, one launch (start us, length us, event | category | flops | bytes accessed | tf_op | source)
XLA Modules:
  0.0 49.3 jit_solution(8323778159727009529)
XLA Ops:
  0.0 2.2 %shard_map.64 = (bf16[1536,256]{1,0:T(8,128)(2,1)S(1)}, f32[48,256]{1,0:T(8,128)S(1)}) custom-call(s32[1]{0:T(128)} %bitcast.place_ref, bf16[1,256,768]{2,1,0:T(8,128)(2,1)} %act_ref.1, f32[1,256,768]{2,1,0:T(8,128)} %filt_ref.1, bf16[2,128,768]{2,1,0:T(8,128)(2,1)} %taps_ref.1, f32[2,768]{1,0:T(2,128)} %gain_ref.1), custom_call_target="tpu_custom_call" | custom-call | tf_op jit(solution)/shard_map/pallas_call | solution.py:288
  2.2 0.0 copy-start
  2.2 0.0 copy-start.1
  2.3 27.1 %all_to_all.10 = bf16[32,48,256]{2,1,0:T(8,128)(2,1)S(1)} all-to-all(bf16[32,48,256]{2,1,0:T(8,128)(2,1)S(1)} %bitcast.8), channel_id=1, replica_groups={{0,8,1,9,2,10,3,11,4,12,5,13,6,14,7,15,16,24,17,25,18,26,19,27,20,28,21..., dimensions={0} | all-to-all | bytes 1572864 | tf_op jit(solution)/shard_map/all_to_all | solution.py:268
  29.3 0.0 copy-done
  29.3 0.0 copy-done.1
  29.4 2.8 %shard_map.65 = bf16[768,256]{1,0:T(8,128)(2,1)S(1)} custom-call(bf16[1536,256]{1,0:T(8,128)(2,1)S(1)} %bitcast.5, f32[48,256]{1,0:T(8,128)S(1)} %get-tuple-element.8.own_ref, f32[40,256]{1,0:T(8,128)S(1)} %copy-done.1, bf16[784,256]{1,0:T(8,128)(2,1)S(1)} %copy-done), custom_call_target="tpu_custom_call" | custom-call | tf_op jit(solution)/shard_map/pallas_call | solution.py:307
  32.1 16.2 %all_to_all.11 = bf16[32,24,256]{2,1,0:T(8,128)(2,1)S(1)} all-to-all(bf16[32,24,256]{2,1,0:T(8,128)(2,1)S(1)} %bitcast.7), channel_id=1, replica_groups={{0,8,1,9,2,10,3,11,4,12,5,13,6,14,7,15,16,24,17,25,18,26,19,27,20,28,21..., dimensions={0} | all-to-all | bytes 786432 | tf_op jit(solution)/shard_map/all_to_all | solution.py:268
  48.3 1.0 %shard_map.66 = bf16[1,256,768]{2,1,0:T(8,128)(2,1)} custom-call(bf16[768,256]{1,0:T(8,128)(2,1)S(1)} %bitcast.6), custom_call_target="tpu_custom_call" | custom-call | tf_op jit(solution)/shard_map/pallas_call | solution.py:315
Async XLA Ops:
  2.2 27.1 %copy-start = (bf16[784,256]{1,0:T(8,128)(2,1)S(1)}, bf16[784,256]{1,0:T(8,128)(2,1)}, u32[]{:S(2)}) copy-start(bf16[784,256]{1,0:T(8,128)(2,1)} %constant.15.clone.table_ref) | copy-start | bytes 1204228
  2.2 27.1 %copy-start.1 = (f32[40,256]{1,0:T(8,128)S(1)}, f32[40,256]{1,0:T(8,128)}, u32[]{:S(2)}) copy-start(f32[40,256]{1,0:T(8,128)} %constant.16.clone.turn_ref) | copy-start | bytes 122884

commit v3 on v1

--- a/solution.py
+++ b/solution.py
@@ -95,7 +95,8 @@
     )
     for copy in arriving:
         copy.start()
-    eye = identity(128)
+    size = math.gcd(act_ref.shape[2], 256)
+    eye = identity(size)
     mine = lax.broadcasted_iota(jnp.int32, (width, channels), 0)
     them = lax.broadcasted_iota(jnp.int32, (width, channels), 1)
     place = jnp.int32(0)
@@ -108,18 +109,25 @@
         gain = jnp.sum(pick * gain_held[s : s + 1, :], axis=1, keepdims=True)
         own_ref[s * width : (s + 1) * width, :length] = dot_rows(pick.astype(jnp.bfloat16), taps_held[s])
         own_ref[s * width : (s + 1) * width, length:] = jnp.broadcast_to(gain, (width, 128))
-    both = []
-    for copy, held in zip(arriving, (act_held, filt_held)):
+    def across(copy, held):
         copy.wait()
-        turned = [
-            dot_rows(eye, held[:, start : start + 128].astype(jnp.bfloat16))
-            for start in range(0, held.shape[1], 128)
+        columns = [
+            dot_rows(eye, held[:, start : start + size].astype(jnp.bfloat16))
+            for start in range(0, held.shape[1], size)
         ]
-        both.append(jnp.concatenate(turned, axis=0))
+        return jnp.concatenate(columns, axis=0)
+
+    even = width // 16 * 16
+    act = across(arriving[0], act_held)
+    for d in range(len(order) if even else 0):
+        start = d * width
+        out_ref[2 * start : 2 * start + even] = act[start : start + even].astype(jnp.bfloat16)
+    filt = across(arriving[1], filt_held)
     for d in range(len(order)):
-        part = slice(d * width, (d + 1) * width)
-        piece = jnp.concatenate([array[part] for array in both], axis=0).astype(jnp.bfloat16)
-        out_ref[2 * d * width : 2 * (d + 1) * width] = piece
+        start, end = d * width, (d + 1) * width
+        parts = [act[start + even : end], filt[start + even : end], filt[start : start + even]]
+        rest = jnp.concatenate([part for part in parts if part.shape[0]], axis=0)
+        out_ref[2 * start + even : 2 * end] = rest.astype(jnp.bfloat16)
 
 
 def final_kernel(in_ref, out_ref):
@@ -233,7 +241,11 @@
         return lr * rr - li * ri, lr * ri + li * rr
 
     chunks = [chunk(s) for s in range(sections)]
-    specs = forward([chunks[0][:, :width]] + [part[:, width:] for part in chunks])
+    odd = 2 * width - width // 16 * 16
+    longs = [jnp.concatenate([part[:, odd:], part[:, width:odd]], axis=1) for part in chunks]
+    if odd == 2 * width:
+        longs = [part[:, width:] for part in chunks]
+    specs = forward([chunks[0][:, :width]] + longs)
     signal_spec = specs[:span]
     results = []
     for s in range(sections):

time: 49.2 us -> 49.3 us (level)
  no operation moved by 1% of the time
where the time goes in v3:
time: 49.3 us; the launch traced here: 49 us
  blocking collectives  43.3 us (88%)
  Pallas kernels  5.74 us (12%)
    all_to_all x2, blocking collectives, exchanged(): lax.all_to_all(chunks, BOTH, split_axis=0, concat_axis=0, tiled=True, axi...  43.3 us
    pallas_call x1, Pallas kernels, body(): pl.pallas_call(functools.partial(main_kernel, width, sections, split, ord...  2.75 us
    pallas_call x1, Pallas kernels, body(): pl.pallas_call(functools.partial(send_kernel, width, owned, order), out_s...  1.94 us
    pallas_call x1, Pallas kernels, body(): pl.pallas_call(final_kernel, out_shape=jax.ShapeDtypeStruct((1, cols, lai...  1.05 us

profile of v3, /device:TPU:0, one launch (start us, length us, event | category | flops | bytes accessed | tf_op | source)
XLA Modules:
  0.0 49.0 jit_solution(13654812267573058487)
XLA Ops:
  0.0 1.9 %shard_map.64 = (bf16[1536,256]{1,0:T(8,128)(2,1)S(1)}, f32[48,256]{1,0:T(8,128)S(1)}) custom-call(s32[1]{0:T(128)} %bitcast.place_ref, bf16[1,256,768]{2,1,0:T(8,128)(2,1)} %act_ref.1, f32[1,256,768]{2,1,0:T(8,128)} %filt_ref.1, bf16[2,128,768]{2,1,0:T(8,128)(2,1)} %taps_ref.1, f32[2,768]{1,0:T(2,128)} %gain_ref.1), custom_call_target="tpu_custom_call" | custom-call | tf_op jit(solution)/shard_map/pallas_call | solution.py:301
  2.0 0.0 copy-start
  2.0 0.0 copy-start.1
  2.0 27.1 %all_to_all.10 = bf16[32,48,256]{2,1,0:T(8,128)(2,1)S(1)} all-to-all(bf16[32,48,256]{2,1,0:T(8,128)(2,1)S(1)} %bitcast.8), channel_id=1, replica_groups={{0,8,1,9,2,10,3,11,4,12,5,13,6,14,7,15,16,24,17,25,18,26,19,27,20,28,21..., dimensions={0} | all-to-all | bytes 1572864 | tf_op jit(solution)/shard_map/all_to_all | solution.py:281
  29.1 0.0 copy-done
  29.1 0.0 copy-done.1
  29.1 2.7 %shard_map.65 = bf16[768,256]{1,0:T(8,128)(2,1)S(1)} custom-call(bf16[1536,256]{1,0:T(8,128)(2,1)S(1)} %bitcast.5, f32[48,256]{1,0:T(8,128)S(1)} %get-tuple-element.8.own_ref, f32[40,256]{1,0:T(8,128)S(1)} %copy-done.1, bf16[784,256]{1,0:T(8,128)(2,1)S(1)} %copy-done), custom_call_target="tpu_custom_call" | custom-call | tf_op jit(solution)/shard_map/pallas_call | solution.py:320
  31.8 16.2 %all_to_all.11 = bf16[32,24,256]{2,1,0:T(8,128)(2,1)S(1)} all-to-all(bf16[32,24,256]{2,1,0:T(8,128)(2,1)S(1)} %bitcast.7), channel_id=1, replica_groups={{0,8,1,9,2,10,3,11,4,12,5,13,6,14,7,15,16,24,17,25,18,26,19,27,20,28,21..., dimensions={0} | all-to-all | bytes 786432 | tf_op jit(solution)/shard_map/all_to_all | solution.py:281
  48.0 1.0 %shard_map.66 = bf16[1,256,768]{2,1,0:T(8,128)(2,1)} custom-call(bf16[768,256]{1,0:T(8,128)(2,1)S(1)} %bitcast.6), custom_call_target="tpu_custom_call" | custom-call | tf_op jit(solution)/shard_map/pallas_call | solution.py:328
Async XLA Ops:
  2.0 27.1 %copy-start = (bf16[784,256]{1,0:T(8,128)(2,1)S(1)}, bf16[784,256]{1,0:T(8,128)(2,1)}, u32[]{:S(2)}) copy-start(bf16[784,256]{1,0:T(8,128)(2,1)} %constant.15.clone.table_ref) | copy-start | bytes 1204228
  2.0 27.1 %copy-start.1 = (f32[40,256]{1,0:T(8,128)S(1)}, f32[40,256]{1,0:T(8,128)}, u32[]{:S(2)}) copy-start(f32[40,256]{1,0:T(8,128)} %constant.16.clone.turn_ref) | copy-start | bytes 122884

commit v4 on v3

--- a/solution.py
+++ b/solution.py
@@ -14,13 +14,20 @@
 MIB = 1024 * 1024
 
 
-def spread_order(devices, seq_devices):
-    half = seq_devices // 2
-    along = [place // 2 + place % 2 * half for place in range(2 * half)]
-    along += range(2 * half, seq_devices)
-    return tuple(
-        start + q for start in range(0, devices, seq_devices) for q in along
-    )
+FIELDS = {2: 7, 3: 11, 4: 19, 5: 37, 6: 67, 7: 131, 8: 285, 9: 529, 10: 1033}
+
+
+def spread_order(devices):
+    bits = devices.bit_length() - 1
+    if devices != 1 << bits or bits not in FIELDS:
+        return tuple(range(devices))
+    order, power = [0], 1
+    while len(order) < devices:
+        order.append(power)
+        power <<= 1
+        if power & devices:
+            power ^= FIELDS[bits]
+    return tuple(order)
 
 
 def tables(real_rows, cols, split):
@@ -95,7 +102,7 @@
     )
     for copy in arriving:
         copy.start()
-    size = math.gcd(act_ref.shape[2], 256)
+    size = 128
     eye = identity(size)
     mine = lax.broadcasted_iota(jnp.int32, (width, channels), 0)
     them = lax.broadcasted_iota(jnp.int32, (width, channels), 1)
@@ -269,7 +276,7 @@
     width = -(-owned // LANES) * LANES
     cols = tokens
     laid = devices * width
-    order = spread_order(devices, seq_devices)
+    order = spread_order(devices)
 
     def widen(array):
         split = array.reshape(array.shape[:2] + (devices, owned))

time: 49.3 us -> 49.4 us (level)
  no operation moved by 1% of the time
where the time goes in v4:
time: 49.4 us; the launch traced here: 49.2 us
  blocking collectives  43.6 us (88%)
  Pallas kernels  5.59 us (11%)
    all_to_all x2, blocking collectives, exchanged(): lax.all_to_all(chunks, BOTH, split_axis=0, concat_axis=0, tiled=True, axi...  43.6 us
    pallas_call x1, Pallas kernels, body(): pl.pallas_call(functools.partial(main_kernel, width, sections, split, ord...  2.73 us
    pallas_call x1, Pallas kernels, body(): pl.pallas_call(functools.partial(send_kernel, width, owned, order), out_s...  1.82 us
    pallas_call x1, Pallas kernels, body(): pl.pallas_call(final_kernel, out_shape=jax.ShapeDtypeStruct((1, cols, lai...  1.05 us

profile of v4, /device:TPU:0, one launch (start us, length us, event | category | flops | bytes accessed | tf_op | source)
XLA Modules:
  0.0 49.2 jit_solution(13172812544122685624)
XLA Ops:
  0.0 1.8 %shard_map.64 = (bf16[1536,256]{1,0:T(8,128)(2,1)S(1)}, f32[48,256]{1,0:T(8,128)S(1)}) custom-call(s32[1]{0:T(128)} %bitcast.place_ref, bf16[1,256,768]{2,1,0:T(8,128)(2,1)} %act_ref.1, f32[1,256,768]{2,1,0:T(8,128)} %filt_ref.1, bf16[2,128,768]{2,1,0:T(8,128)(2,1)} %taps_ref.1, f32[2,768]{1,0:T(2,128)} %gain_ref.1), custom_call_target="tpu_custom_call" | custom-call | tf_op jit(solution)/shard_map/pallas_call | solution.py:308
  1.8 0.0 copy-start
  1.8 0.0 copy-start.1
  1.9 26.1 %all_to_all.10 = bf16[32,48,256]{2,1,0:T(8,128)(2,1)S(1)} all-to-all(bf16[32,48,256]{2,1,0:T(8,128)(2,1)S(1)} %bitcast.8), channel_id=1, replica_groups={{0,1,2,4,8,16,5,10,20,13,26,17,7,14,28,29,31,27,19,3,6,12,24,21,15,30,2..., dimensions={0} | all-to-all | bytes 1572864 | tf_op jit(solution)/shard_map/all_to_all | solution.py:288
  27.9 0.0 copy-done
  27.9 0.0 copy-done.1
  27.9 2.7 %shard_map.65 = bf16[768,256]{1,0:T(8,128)(2,1)S(1)} custom-call(bf16[1536,256]{1,0:T(8,128)(2,1)S(1)} %bitcast.5, f32[48,256]{1,0:T(8,128)S(1)} %get-tuple-element.8.own_ref, f32[40,256]{1,0:T(8,128)S(1)} %copy-done.1, bf16[784,256]{1,0:T(8,128)(2,1)S(1)} %copy-done), custom_call_target="tpu_custom_call" | custom-call | tf_op jit(solution)/shard_map/pallas_call | solution.py:327
  30.7 17.5 %all_to_all.11 = bf16[32,24,256]{2,1,0:T(8,128)(2,1)S(1)} all-to-all(bf16[32,24,256]{2,1,0:T(8,128)(2,1)S(1)} %bitcast.7), channel_id=1, replica_groups={{0,1,2,4,8,16,5,10,20,13,26,17,7,14,28,29,31,27,19,3,6,12,24,21,15,30,2..., dimensions={0} | all-to-all | bytes 786432 | tf_op jit(solution)/shard_map/all_to_all | solution.py:288
  48.2 1.0 %shard_map.66 = bf16[1,256,768]{2,1,0:T(8,128)(2,1)} custom-call(bf16[768,256]{1,0:T(8,128)(2,1)S(1)} %bitcast.6), custom_call_target="tpu_custom_call" | custom-call | tf_op jit(solution)/shard_map/pallas_call | solution.py:335
Async XLA Ops:
  1.8 26.1 %copy-start = (bf16[784,256]{1,0:T(8,128)(2,1)S(1)}, bf16[784,256]{1,0:T(8,128)(2,1)}, u32[]{:S(2)}) copy-start(bf16[784,256]{1,0:T(8,128)(2,1)} %constant.15.clone.table_ref) | copy-start | bytes 1204228
  1.8 26.1 %copy-start.1 = (f32[40,256]{1,0:T(8,128)S(1)}, f32[40,256]{1,0:T(8,128)}, u32[]{:S(2)}) copy-start(f32[40,256]{1,0:T(8,128)} %constant.16.clone.turn_ref) | copy-start | bytes 122884

commit v5 on v4

--- a/solution.py
+++ b/solution.py
@@ -48,7 +48,9 @@
     parts = [np.block([[c, -s], [s, c]]), row_part]
     lanes = max(part.shape[1] for part in parts)
     stacked = np.concatenate([np.pad(p, ((0, 0), (0, lanes - p.shape[1]))) for p in parts])
-    return jnp.asarray(stacked, jnp.bfloat16), jnp.asarray(turn, jnp.float32)
+    back = np.kron(first.reshape(2, freqs, real_rows)[:, 1:].reshape(-1, real_rows).T, np.eye(LANES))
+    bf = jnp.bfloat16
+    return jnp.asarray(stacked, bf), jnp.asarray(back, bf), jnp.asarray(turn, jnp.float32)
 
 
 def dot(a, b):
@@ -146,7 +148,7 @@
         out_ref[0, :, part] = dot_rows(eye, in_ref[part]).astype(jnp.bfloat16)
 
 
-def main_kernel(width, sections, split, order, in_ref, own_ref, turn_ref, table_ref, out_ref):
+def main_kernel(width, sections, split, order, in_ref, own_ref, turn_ref, table_ref, back_ref, out_ref):
     total, tokens = in_ref.shape
     cols = tokens // split
     seq = total // (2 * width * sections)
@@ -170,16 +172,12 @@
         [jnp.concatenate([level, plus], axis=1), jnp.concatenate([minus, level], axis=1)], axis=0
     )
     forward_rows = table_ref[2 * cols : 2 * cols + 2 * high, : rows * LANES]
-    wide_rows = forward_rows.astype(jnp.float32)
-    some_rows = jnp.concatenate([wide_rows[LANES:high], wide_rows[high + LANES :]], axis=0)
-    back_rows = dot_rows(identity(rows * LANES), some_rows.astype(bf)).astype(bf)
-
     def chunk(s):
         starts = [order.index(s * seq + q) * 2 * width for q in range(seq)]
         part = jnp.concatenate([in_ref[at : at + 2 * width] for at in starts], axis=0)
         return part.astype(jnp.float32).reshape(seq, 2 * width, tokens)
 
-    def forward(grids):
+    def forward(grids, others=()):
         blocks = []
         for grid in grids:
             for g in range(groups):
@@ -194,7 +192,7 @@
             turned.append(
                 jnp.concatenate([real * cosine + imag * sine, imag * cosine - real * sine], axis=1)
             )
-        return dot(jnp.concatenate(turned, axis=0).astype(bf), forward_cols)
+        return dot(jnp.concatenate(turned + list(others), axis=0).astype(bf), forward_cols)
 
     def times(left, right):
         lr, li = left[:, :cols], left[:, cols:]
@@ -210,7 +208,7 @@
         for g in range(groups):
             part = slice(g * high + LANES, (g + 1) * high)
             joined.append(jnp.concatenate([turned_real[part], turned_imag[part]], axis=0))
-        spread = dot(back_rows, jnp.concatenate(joined, axis=1).astype(bf))
+        spread = dot(back_ref[...], jnp.concatenate(joined, axis=1).astype(bf))
         pieces = []
         for g in range(groups):
             piece = spread[:, g * cols : (g + 1) * cols].reshape(rows, LANES, cols)
@@ -219,22 +217,20 @@
             pieces.append(jnp.concatenate(parts, axis=2))
         return jnp.concatenate(pieces, axis=1)
 
-    def short_specs():
+    def short_blocks():
+        none = [jnp.zeros((high, cols - length), jnp.float32)] if cols > length else []
         turned = []
         for s in range(sections):
             for g in range(groups):
                 start = s * width + g * LANES
                 taps = jnp.concatenate([own_ref[start : start + LANES, :length]] * copies, axis=0)
-                turned.append(
-                    jnp.concatenate([taps * short_cos, taps * short_sin], axis=1)
-                )
-        columns = jnp.concatenate([table_ref[:length, : 2 * cols], table_ref[cols : cols + length, : 2 * cols]])
-        return dot(jnp.concatenate(turned, axis=0).astype(bf), columns)
+                parts = [taps * short_cos] + none + [taps * short_sin] + none
+                turned.append(jnp.concatenate(parts, axis=1))
+        return turned
 
     row = lax.broadcasted_iota(jnp.int32, (high, 1), 0)
     weight = jnp.where(row < LANES, scale / whole, 2.0 * scale / whole)
     short_cos, short_sin = cosine[:, :length] * weight, -(sine[:, :length] * weight)
-    shorts = short_specs()
 
     def combine(s, spec):
         gains = own_ref[s * width : (s + 1) * width, length:] * (1.0 / scale)
@@ -252,7 +248,8 @@
     longs = [jnp.concatenate([part[:, odd:], part[:, width:odd]], axis=1) for part in chunks]
     if odd == 2 * width:
         longs = [part[:, width:] for part in chunks]
-    specs = forward([chunks[0][:, :width]] + longs)
+    specs = forward([chunks[0][:, :width]] + longs, short_blocks())
+    shorts = specs[(sections + 1) * span :]
     signal_spec = specs[:span]
     results = []
     for s in range(sections):
@@ -297,7 +294,7 @@
     if width != owned:
         acts, filters = widen(acts), widen(filters)
     split = 2 if seq_devices <= 32 and cols % 256 == 0 else 1
-    table, turn = tables(seq_devices * split, cols // split, split)
+    table, back_table, turn = tables(seq_devices * split, cols // split, split)
     vmem = pl.BlockSpec(memory_space=pltpu.VMEM)
     hbm = pl.BlockSpec(memory_space=pltpu.HBM)
     area = laid * cols
@@ -327,10 +324,10 @@
     results = pl.pallas_call(
         functools.partial(main_kernel, width, sections, split, order),
         out_shape=jax.ShapeDtypeStruct((laid, cols), jnp.bfloat16),
-        in_specs=[vmem] * 4,
+        in_specs=[vmem] * 5,
         out_specs=vmem,
-        compiler_params=grant(2 * MIB + 6 * area + 2 * table.size + 64 * span * cols),
-    )(arrived, own, turn, table)
+        compiler_params=grant(2 * MIB + 6 * area + 2 * table.size + 2 * back_table.size + 64 * span * cols),
+    )(arrived, own, turn, table, back_table)
     returned = exchanged(results, width)
     final = pl.pallas_call(
         final_kernel,

time: 49.4 us -> 49.6 us (level)
  no operation moved by 1% of the time
where the time goes in v5:
time: 49.6 us; the launch traced here: 49.4 us
  blocking collectives  43.6 us (88%)
  Pallas kernels  5.77 us (12%)
    all_to_all x2, blocking collectives, exchanged(): lax.all_to_all(chunks, BOTH, split_axis=0, concat_axis=0, tiled=True, axi...  43.6 us
    pallas_call x1, Pallas kernels, body(): pl.pallas_call(functools.partial(main_kernel, width, sections, split, ord...  2.91 us
    pallas_call x1, Pallas kernels, body(): pl.pallas_call(functools.partial(send_kernel, width, owned, order), out_s...  1.82 us
    pallas_call x1, Pallas kernels, body(): pl.pallas_call(final_kernel, out_shape=jax.ShapeDtypeStruct((1, cols, lai...  1.05 us

profile of v5, /device:TPU:0, one launch (start us, length us, event | category | flops | bytes accessed | tf_op | source)
XLA Modules:
  0.0 49.4 jit_solution(18360139908925189340)
XLA Ops:
  0.0 1.8 %shard_map.73 = (bf16[1536,256]{1,0:T(8,128)(2,1)S(1)}, f32[48,256]{1,0:T(8,128)S(1)}) custom-call(s32[1]{0:T(128)} %bitcast.place_ref, bf16[1,256,768]{2,1,0:T(8,128)(2,1)} %act_ref.1, f32[1,256,768]{2,1,0:T(8,128)} %filt_ref.1, bf16[2,128,768]{2,1,0:T(8,128)(2,1)} %taps_ref.1, f32[2,768]{1,0:T(2,128)} %gain_ref.1), custom_call_target="tpu_custom_call" | custom-call | tf_op jit(solution)/shard_map/pallas_call | solution.py:305
  1.8 0.0 copy-start
  1.8 0.0 copy-start.1
  1.9 0.0 copy-start.2
  1.9 26.1 %all_to_all.10 = bf16[32,48,256]{2,1,0:T(8,128)(2,1)S(1)} all-to-all(bf16[32,48,256]{2,1,0:T(8,128)(2,1)S(1)} %bitcast.8), channel_id=1, replica_groups={{0,1,2,4,8,16,5,10,20,13,26,17,7,14,28,29,31,27,19,3,6,12,24,21,15,30,2..., dimensions={0} | all-to-all | bytes 1572864 | tf_op jit(solution)/shard_map/all_to_all | solution.py:285
  28.0 0.0 copy-done
  28.0 0.0 copy-done.1
  28.0 0.0 copy-done.2
  28.0 2.9 %shard_map.74 = bf16[768,256]{1,0:T(8,128)(2,1)S(1)} custom-call(bf16[1536,256]{1,0:T(8,128)(2,1)S(1)} %bitcast.5, f32[48,256]{1,0:T(8,128)S(1)} %get-tuple-element.8.own_ref, f32[40,256]{1,0:T(8,128)S(1)} %copy-done.2, bf16[784,256]{1,0:T(8,128)(2,1)S(1)} %copy-done, bf16[256,512]{1,0:T(8,128)(2,1)S(1)} %copy-done.1), custom_call_target="tpu_custom_call" | custom-call | tf_op jit(solution)/shard_map/pallas_call | solution.py:324
  30.9 17.5 %all_to_all.11 = bf16[32,24,256]{2,1,0:T(8,128)(2,1)S(1)} all-to-all(bf16[32,24,256]{2,1,0:T(8,128)(2,1)S(1)} %bitcast.7), channel_id=1, replica_groups={{0,1,2,4,8,16,5,10,20,13,26,17,7,14,28,29,31,27,19,3,6,12,24,21,15,30,2..., dimensions={0} | all-to-all | bytes 786432 | tf_op jit(solution)/shard_map/all_to_all | solution.py:285
  48.4 1.0 %shard_map.75 = bf16[1,256,768]{2,1,0:T(8,128)(2,1)} custom-call(bf16[768,256]{1,0:T(8,128)(2,1)S(1)} %bitcast.6), custom_call_target="tpu_custom_call" | custom-call | tf_op jit(solution)/shard_map/pallas_call | solution.py:332
Async XLA Ops:
  1.8 26.1 %copy-start = (bf16[784,256]{1,0:T(8,128)(2,1)S(1)}, bf16[784,256]{1,0:T(8,128)(2,1)}, u32[]{:S(2)}) copy-start(bf16[784,256]{1,0:T(8,128)(2,1)} %constant.17.clone.table_ref) | copy-start | bytes 1204228
  1.8 26.1 %copy-start.1 = (bf16[256,512]{1,0:T(8,128)(2,1)S(1)}, bf16[256,512]{1,0:T(8,128)(2,1)}, u32[]{:S(2)}) copy-start(bf16[256,512]{1,0:T(8,128)(2,1)} %constant.18.clone.back_ref) | copy-start | bytes 786436
  1.9 26.1 %copy-start.2 = (f32[40,256]{1,0:T(8,128)S(1)}, f32[40,256]{1,0:T(8,128)}, u32[]{:S(2)}) copy-start(f32[40,256]{1,0:T(8,128)} %constant.19.clone.turn_ref) | copy-start | bytes 122884

commit v6 on v3

--- a/solution.py
+++ b/solution.py
@@ -41,7 +41,9 @@
     parts = [np.block([[c, -s], [s, c]]), row_part]
     lanes = max(part.shape[1] for part in parts)
     stacked = np.concatenate([np.pad(p, ((0, 0), (0, lanes - p.shape[1]))) for p in parts])
-    return jnp.asarray(stacked, jnp.bfloat16), jnp.asarray(turn, jnp.float32)
+    back = np.kron(first.reshape(2, freqs, real_rows)[:, 1:].reshape(-1, real_rows).T, np.eye(LANES))
+    bf = jnp.bfloat16
+    return jnp.asarray(stacked, bf), jnp.asarray(back, bf), jnp.asarray(turn, jnp.float32)
 
 
 def dot(a, b):
@@ -95,7 +97,7 @@
     )
     for copy in arriving:
         copy.start()
-    size = math.gcd(act_ref.shape[2], 256)
+    size = 128
     eye = identity(size)
     mine = lax.broadcasted_iota(jnp.int32, (width, channels), 0)
     them = lax.broadcasted_iota(jnp.int32, (width, channels), 1)
@@ -139,7 +141,7 @@
         out_ref[0, :, part] = dot_rows(eye, in_ref[part]).astype(jnp.bfloat16)
 
 
-def main_kernel(width, sections, split, order, in_ref, own_ref, turn_ref, table_ref, out_ref):
+def main_kernel(width, sections, split, order, in_ref, own_ref, turn_ref, table_ref, back_ref, out_ref):
     total, tokens = in_ref.shape
     cols = tokens // split
     seq = total // (2 * width * sections)
@@ -163,10 +165,6 @@
         [jnp.concatenate([level, plus], axis=1), jnp.concatenate([minus, level], axis=1)], axis=0
     )
     forward_rows = table_ref[2 * cols : 2 * cols + 2 * high, : rows * LANES]
-    wide_rows = forward_rows.astype(jnp.float32)
-    some_rows = jnp.concatenate([wide_rows[LANES:high], wide_rows[high + LANES :]], axis=0)
-    back_rows = dot_rows(identity(rows * LANES), some_rows.astype(bf)).astype(bf)
-
     def chunk(s):
         starts = [order.index(s * seq + q) * 2 * width for q in range(seq)]
         part = jnp.concatenate([in_ref[at : at + 2 * width] for at in starts], axis=0)
@@ -203,7 +201,7 @@
         for g in range(groups):
             part = slice(g * high + LANES, (g + 1) * high)
             joined.append(jnp.concatenate([turned_real[part], turned_imag[part]], axis=0))
-        spread = dot(back_rows, jnp.concatenate(joined, axis=1).astype(bf))
+        spread = dot(back_ref[...], jnp.concatenate(joined, axis=1).astype(bf))
         pieces = []
         for g in range(groups):
             piece = spread[:, g * cols : (g + 1) * cols].reshape(rows, LANES, cols)
@@ -290,7 +288,7 @@
     if width != owned:
         acts, filters = widen(acts), widen(filters)
     split = 2 if seq_devices <= 32 and cols % 256 == 0 else 1
-    table, turn = tables(seq_devices * split, cols // split, split)
+    table, back_table, turn = tables(seq_devices * split, cols // split, split)
     vmem = pl.BlockSpec(memory_space=pltpu.VMEM)
     hbm = pl.BlockSpec(memory_space=pltpu.HBM)
     area = laid * cols
@@ -320,10 +318,10 @@
     results = pl.pallas_call(
         functools.partial(main_kernel, width, sections, split, order),
         out_shape=jax.ShapeDtypeStruct((laid, cols), jnp.bfloat16),
-        in_specs=[vmem] * 4,
+        in_specs=[vmem] * 5,
         out_specs=vmem,
-        compiler_params=grant(2 * MIB + 6 * area + 2 * table.size + 64 * span * cols),
-    )(arrived, own, turn, table)
+        compiler_params=grant(2 * MIB + 6 * area + 2 * table.size + 2 * back_table.size + 64 * span * cols),
+    )(arrived, own, turn, table, back_table)
     returned = exchanged(results, width)
     final = pl.pallas_call(
         final_kernel,

time: 49.3 us -> 49.1 us (level)
  no operation moved by 1% of the time
where the time goes in v6:
time: 49.1 us; the launch traced here: 48.8 us
  blocking collectives  43.3 us (88%)
  Pallas kernels  5.51 us (11%)
    all_to_all x2, blocking collectives, exchanged(): lax.all_to_all(chunks, BOTH, split_axis=0, concat_axis=0, tiled=True, axi...  43.3 us
    pallas_call x1, Pallas kernels, body(): pl.pallas_call(functools.partial(main_kernel, width, sections, split, ord...  2.65 us
    pallas_call x1, Pallas kernels, body(): pl.pallas_call(functools.partial(send_kernel, width, owned, order), out_s...  1.82 us
    pallas_call x1, Pallas kernels, body(): pl.pallas_call(final_kernel, out_shape=jax.ShapeDtypeStruct((1, cols, lai...  1.04 us

profile of v6, /device:TPU:0, one launch (start us, length us, event | category | flops | bytes accessed | tf_op | source)
XLA Modules:
  0.0 48.8 jit_solution(10871931905974836468)
XLA Ops:
  0.0 1.8 %shard_map.73 = (bf16[1536,256]{1,0:T(8,128)(2,1)S(1)}, f32[48,256]{1,0:T(8,128)S(1)}) custom-call(s32[1]{0:T(128)} %bitcast.place_ref, bf16[1,256,768]{2,1,0:T(8,128)(2,1)} %act_ref.1, f32[1,256,768]{2,1,0:T(8,128)} %filt_ref.1, bf16[2,128,768]{2,1,0:T(8,128)(2,1)} %taps_ref.1, f32[2,768]{1,0:T(2,128)} %gain_ref.1), custom_call_target="tpu_custom_call" | custom-call | tf_op jit(solution)/shard_map/pallas_call | solution.py:299
  1.8 0.0 copy-start
  1.8 0.0 copy-start.1
  1.9 0.0 copy-start.2
  1.9 27.1 %all_to_all.10 = bf16[32,48,256]{2,1,0:T(8,128)(2,1)S(1)} all-to-all(bf16[32,48,256]{2,1,0:T(8,128)(2,1)S(1)} %bitcast.8), channel_id=1, replica_groups={{0,8,1,9,2,10,3,11,4,12,5,13,6,14,7,15,16,24,17,25,18,26,19,27,20,28,21..., dimensions={0} | all-to-all | bytes 1572864 | tf_op jit(solution)/shard_map/all_to_all | solution.py:279
  29.0 0.0 copy-done
  29.0 0.0 copy-done.1
  29.0 0.0 copy-done.2
  29.0 2.6 %shard_map.74 = bf16[768,256]{1,0:T(8,128)(2,1)S(1)} custom-call(bf16[1536,256]{1,0:T(8,128)(2,1)S(1)} %bitcast.5, f32[48,256]{1,0:T(8,128)S(1)} %get-tuple-element.8.own_ref, f32[40,256]{1,0:T(8,128)S(1)} %copy-done.2, bf16[784,256]{1,0:T(8,128)(2,1)S(1)} %copy-done, bf16[256,512]{1,0:T(8,128)(2,1)S(1)} %copy-done.1), custom_call_target="tpu_custom_call" | custom-call | tf_op jit(solution)/shard_map/pallas_call | solution.py:318
  31.6 16.2 %all_to_all.11 = bf16[32,24,256]{2,1,0:T(8,128)(2,1)S(1)} all-to-all(bf16[32,24,256]{2,1,0:T(8,128)(2,1)S(1)} %bitcast.7), channel_id=1, replica_groups={{0,8,1,9,2,10,3,11,4,12,5,13,6,14,7,15,16,24,17,25,18,26,19,27,20,28,21..., dimensions={0} | all-to-all | bytes 786432 | tf_op jit(solution)/shard_map/all_to_all | solution.py:279
  47.8 1.0 %shard_map.75 = bf16[1,256,768]{2,1,0:T(8,128)(2,1)} custom-call(bf16[768,256]{1,0:T(8,128)(2,1)S(1)} %bitcast.6), custom_call_target="tpu_custom_call" | custom-call | tf_op jit(solution)/shard_map/pallas_call | solution.py:326
Async XLA Ops:
  1.8 27.1 %copy-start = (bf16[784,256]{1,0:T(8,128)(2,1)S(1)}, bf16[784,256]{1,0:T(8,128)(2,1)}, u32[]{:S(2)}) copy-start(bf16[784,256]{1,0:T(8,128)(2,1)} %constant.17.clone.table_ref) | copy-start | bytes 1204228
  1.8 27.1 %copy-start.1 = (bf16[256,512]{1,0:T(8,128)(2,1)S(1)}, bf16[256,512]{1,0:T(8,128)(2,1)}, u32[]{:S(2)}) copy-start(bf16[256,512]{1,0:T(8,128)(2,1)} %constant.18.clone.back_ref) | copy-start | bytes 786436
  1.9 27.1 %copy-start.2 = (f32[40,256]{1,0:T(8,128)S(1)}, f32[40,256]{1,0:T(8,128)}, u32[]{:S(2)}) copy-start(f32[40,256]{1,0:T(8,128)} %constant.19.clone.turn_ref) | copy-start | bytes 122884

commit v7 on v6

--- a/solution.py
+++ b/solution.py
@@ -210,30 +210,25 @@
             pieces.append(jnp.concatenate(parts, axis=2))
         return jnp.concatenate(pieces, axis=1)
 
-    def short_specs():
+    def short_spec(s):
         turned = []
-        for s in range(sections):
-            for g in range(groups):
-                start = s * width + g * LANES
-                taps = jnp.concatenate([own_ref[start : start + LANES, :length]] * copies, axis=0)
-                turned.append(
-                    jnp.concatenate([taps * short_cos, taps * short_sin], axis=1)
-                )
+        for g in range(groups):
+            start = s * width + g * LANES
+            taps = jnp.concatenate([own_ref[start : start + LANES, :length]] * copies, axis=0)
+            turned.append(jnp.concatenate([taps * short_cos, taps * short_sin], axis=1))
         columns = jnp.concatenate([table_ref[:length, : 2 * cols], table_ref[cols : cols + length, : 2 * cols]])
         return dot(jnp.concatenate(turned, axis=0).astype(bf), columns)
 
     row = lax.broadcasted_iota(jnp.int32, (high, 1), 0)
     weight = jnp.where(row < LANES, scale / whole, 2.0 * scale / whole)
     short_cos, short_sin = cosine[:, :length] * weight, -(sine[:, :length] * weight)
-    shorts = short_specs()
-
-    def combine(s, spec):
+
+    def combine(s, short, spec):
         gains = own_ref[s * width : (s + 1) * width, length:] * (1.0 / scale)
         gains = jnp.concatenate([gains] * (cols // 128), axis=1)
         shift = jnp.concatenate(
             [gains[g * LANES : (g + 1) * LANES] for g in range(groups) for _ in range(copies)], axis=0
         )
-        short = shorts[s * span : (s + 1) * span]
         lr, li = spec[:, :cols] + shift, spec[:, cols:]
         rr, ri = short[:, :cols], short[:, cols:]
         return lr * rr - li * ri, lr * ri + li * rr
@@ -243,12 +238,15 @@
     longs = [jnp.concatenate([part[:, odd:], part[:, width:odd]], axis=1) for part in chunks]
     if odd == 2 * width:
         longs = [part[:, width:] for part in chunks]
-    specs = forward([chunks[0][:, :width]] + longs)
+    specs = forward([chunks[0][:, :width], longs[0]])
     signal_spec = specs[:span]
+    filters = combine(0, short_spec(0), specs[span:])
     results = []
     for s in range(sections):
-        mixed = combine(s, specs[(s + 1) * span : (s + 2) * span])
-        result = back(times(signal_spec, mixed))
+        product = times(signal_spec, filters)
+        if s + 1 < sections:
+            filters = combine(s + 1, short_spec(s + 1), forward([longs[s + 1]]))
+        result = back(product)
         results.append(result)
         if s + 1 < sections:
             rounded = result.astype(bf).astype(jnp.float32)

time: 49.1 us -> 49.1 us (level)
  no operation moved by 1% of the time
where the time goes in v7:
time: 49.1 us; the launch traced here: 48.8 us
  blocking collectives  43.3 us (88%)
  Pallas kernels  5.46 us (11%)
    all_to_all x2, blocking collectives, exchanged(): lax.all_to_all(chunks, BOTH, split_axis=0, concat_axis=0, tiled=True, axi...  43.3 us
    pallas_call x1, Pallas kernels, body(): pl.pallas_call(functools.partial(main_kernel, width, sections, split, ord...  2.59 us
    pallas_call x1, Pallas kernels, body(): pl.pallas_call(functools.partial(send_kernel, width, owned, order), out_s...  1.82 us
    pallas_call x1, Pallas kernels, body(): pl.pallas_call(final_kernel, out_shape=jax.ShapeDtypeStruct((1, cols, lai...  1.04 us

profile of v7, /device:TPU:0, one launch (start us, length us, event | category | flops | bytes accessed | tf_op | source)
XLA Modules:
  0.0 48.8 jit_solution(10397472704196658427)
XLA Ops:
  0.0 1.8 %shard_map.73 = (bf16[1536,256]{1,0:T(8,128)(2,1)S(1)}, f32[48,256]{1,0:T(8,128)S(1)}) custom-call(s32[1]{0:T(128)} %bitcast.place_ref, bf16[1,256,768]{2,1,0:T(8,128)(2,1)} %act_ref.1, f32[1,256,768]{2,1,0:T(8,128)} %filt_ref.1, bf16[2,128,768]{2,1,0:T(8,128)(2,1)} %taps_ref.1, f32[2,768]{1,0:T(2,128)} %gain_ref.1), custom_call_target="tpu_custom_call" | custom-call | tf_op jit(solution)/shard_map/pallas_call | solution.py:297
  1.8 0.0 copy-start
  1.8 0.0 copy-start.1
  1.9 0.0 copy-start.2
  1.9 27.1 %all_to_all.10 = bf16[32,48,256]{2,1,0:T(8,128)(2,1)S(1)} all-to-all(bf16[32,48,256]{2,1,0:T(8,128)(2,1)S(1)} %bitcast.8), channel_id=1, replica_groups={{0,8,1,9,2,10,3,11,4,12,5,13,6,14,7,15,16,24,17,25,18,26,19,27,20,28,21..., dimensions={0} | all-to-all | bytes 1572864 | tf_op jit(solution)/shard_map/all_to_all | solution.py:277
  29.0 0.0 copy-done
  29.0 0.0 copy-done.1
  29.0 0.0 copy-done.2
  29.0 2.6 %shard_map.74 = bf16[768,256]{1,0:T(8,128)(2,1)S(1)} custom-call(bf16[1536,256]{1,0:T(8,128)(2,1)S(1)} %bitcast.5, f32[48,256]{1,0:T(8,128)S(1)} %get-tuple-element.8.own_ref, f32[40,256]{1,0:T(8,128)S(1)} %copy-done.2, bf16[784,256]{1,0:T(8,128)(2,1)S(1)} %copy-done, bf16[256,512]{1,0:T(8,128)(2,1)S(1)} %copy-done.1), custom_call_target="tpu_custom_call" | custom-call | tf_op jit(solution)/shard_map/pallas_call | solution.py:316
  31.6 16.2 %all_to_all.11 = bf16[32,24,256]{2,1,0:T(8,128)(2,1)S(1)} all-to-all(bf16[32,24,256]{2,1,0:T(8,128)(2,1)S(1)} %bitcast.7), channel_id=1, replica_groups={{0,8,1,9,2,10,3,11,4,12,5,13,6,14,7,15,16,24,17,25,18,26,19,27,20,28,21..., dimensions={0} | all-to-all | bytes 786432 | tf_op jit(solution)/shard_map/all_to_all | solution.py:277
  47.7 1.0 %shard_map.75 = bf16[1,256,768]{2,1,0:T(8,128)(2,1)} custom-call(bf16[768,256]{1,0:T(8,128)(2,1)S(1)} %bitcast.6), custom_call_target="tpu_custom_call" | custom-call | tf_op jit(solution)/shard_map/pallas_call | solution.py:324
Async XLA Ops:
  1.8 27.1 %copy-start = (bf16[784,256]{1,0:T(8,128)(2,1)S(1)}, bf16[784,256]{1,0:T(8,128)(2,1)}, u32[]{:S(2)}) copy-start(bf16[784,256]{1,0:T(8,128)(2,1)} %constant.17.clone.table_ref) | copy-start | bytes 1204228
  1.8 27.1 %copy-start.1 = (bf16[256,512]{1,0:T(8,128)(2,1)S(1)}, bf16[256,512]{1,0:T(8,128)(2,1)}, u32[]{:S(2)}) copy-start(bf16[256,512]{1,0:T(8,128)(2,1)} %constant.18.clone.back_ref) | copy-start | bytes 786436
  1.9 27.1 %copy-start.2 = (f32[40,256]{1,0:T(8,128)S(1)}, f32[40,256]{1,0:T(8,128)}, u32[]{:S(2)}) copy-start(f32[40,256]{1,0:T(8,128)} %constant.19.clone.turn_ref) | copy-start | bytes 122884

commit v8 on v7

--- a/solution.py
+++ b/solution.py
@@ -248,12 +248,14 @@
             filters = combine(s + 1, short_spec(s + 1), forward([longs[s + 1]]))
         result = back(product)
         results.append(result)
+        for at in range(0, len(order), 2):
+            pair = order[at : at + 2]
+            if max(pair) // seq == s:
+                rows_out = jnp.concatenate([results[rank // seq][rank % seq] for rank in pair], axis=0)
+                out_ref[at * width : (at + 2) * width] = rows_out.astype(bf)
         if s + 1 < sections:
             rounded = result.astype(bf).astype(jnp.float32)
             signal_spec = forward([rounded * chunks[s + 1][:, :width]])
-    for at in range(0, len(order), 2):
-        pair = [results[rank // seq][rank % seq] for rank in order[at : at + 2]]
-        out_ref[at * width : (at + 2) * width] = jnp.concatenate(pair, axis=0).astype(bf)
 
 
 def body(activations, short_filters, long_filters, skip_gain):

time: 49.1 us -> 49.1 us (level)
  no operation moved by 1% of the time
where the time goes in v8:
time: 49.1 us; the launch traced here: 48.8 us
  blocking collectives  43.3 us (88%)
  Pallas kernels  5.46 us (11%)
    all_to_all x2, blocking collectives, exchanged(): lax.all_to_all(chunks, BOTH, split_axis=0, concat_axis=0, tiled=True, axi...  43.3 us
    pallas_call x1, Pallas kernels, body(): pl.pallas_call(functools.partial(main_kernel, width, sections, split, ord...  2.6 us
    pallas_call x1, Pallas kernels, body(): pl.pallas_call(functools.partial(send_kernel, width, owned, order), out_s...  1.82 us
    pallas_call x1, Pallas kernels, body(): pl.pallas_call(final_kernel, out_shape=jax.ShapeDtypeStruct((1, cols, lai...  1.05 us

profile of v8, /device:TPU:0, one launch (start us, length us, event | category | flops | bytes accessed | tf_op | source)
XLA Modules:
  0.0 48.8 jit_solution(4258877003391996217)
XLA Ops:
  0.0 1.8 %shard_map.73 = (bf16[1536,256]{1,0:T(8,128)(2,1)S(1)}, f32[48,256]{1,0:T(8,128)S(1)}) custom-call(s32[1]{0:T(128)} %bitcast.place_ref, bf16[1,256,768]{2,1,0:T(8,128)(2,1)} %act_ref.1, f32[1,256,768]{2,1,0:T(8,128)} %filt_ref.1, bf16[2,128,768]{2,1,0:T(8,128)(2,1)} %taps_ref.1, f32[2,768]{1,0:T(2,128)} %gain_ref.1), custom_call_target="tpu_custom_call" | custom-call | tf_op jit(solution)/shard_map/pallas_call | solution.py:299
  1.8 0.0 copy-start
  1.8 0.0 copy-start.1
  1.9 0.0 copy-start.2
  1.9 27.1 %all_to_all.10 = bf16[32,48,256]{2,1,0:T(8,128)(2,1)S(1)} all-to-all(bf16[32,48,256]{2,1,0:T(8,128)(2,1)S(1)} %bitcast.8), channel_id=1, replica_groups={{0,8,1,9,2,10,3,11,4,12,5,13,6,14,7,15,16,24,17,25,18,26,19,27,20,28,21..., dimensions={0} | all-to-all | bytes 1572864 | tf_op jit(solution)/shard_map/all_to_all | solution.py:279
  29.0 0.0 copy-done
  29.0 0.0 copy-done.1
  29.0 0.0 copy-done.2
  29.0 2.6 %shard_map.74 = bf16[768,256]{1,0:T(8,128)(2,1)S(1)} custom-call(bf16[1536,256]{1,0:T(8,128)(2,1)S(1)} %bitcast.5, f32[48,256]{1,0:T(8,128)S(1)} %get-tuple-element.8.own_ref, f32[40,256]{1,0:T(8,128)S(1)} %copy-done.2, bf16[784,256]{1,0:T(8,128)(2,1)S(1)} %copy-done, bf16[256,512]{1,0:T(8,128)(2,1)S(1)} %copy-done.1), custom_call_target="tpu_custom_call" | custom-call | tf_op jit(solution)/shard_map/pallas_call | solution.py:318
  31.6 16.2 %all_to_all.11 = bf16[32,24,256]{2,1,0:T(8,128)(2,1)S(1)} all-to-all(bf16[32,24,256]{2,1,0:T(8,128)(2,1)S(1)} %bitcast.7), channel_id=1, replica_groups={{0,8,1,9,2,10,3,11,4,12,5,13,6,14,7,15,16,24,17,25,18,26,19,27,20,28,21..., dimensions={0} | all-to-all | bytes 786432 | tf_op jit(solution)/shard_map/all_to_all | solution.py:279
  47.7 1.0 %shard_map.75 = bf16[1,256,768]{2,1,0:T(8,128)(2,1)} custom-call(bf16[768,256]{1,0:T(8,128)(2,1)S(1)} %bitcast.6), custom_call_target="tpu_custom_call" | custom-call | tf_op jit(solution)/shard_map/pallas_call | solution.py:326
Async XLA Ops:
  1.8 27.1 %copy-start = (bf16[784,256]{1,0:T(8,128)(2,1)S(1)}, bf16[784,256]{1,0:T(8,128)(2,1)}, u32[]{:S(2)}) copy-start(bf16[784,256]{1,0:T(8,128)(2,1)} %constant.17.clone.table_ref) | copy-start | bytes 1204228
  1.8 27.1 %copy-start.1 = (bf16[256,512]{1,0:T(8,128)(2,1)S(1)}, bf16[256,512]{1,0:T(8,128)(2,1)}, u32[]{:S(2)}) copy-start(bf16[256,512]{1,0:T(8,128)(2,1)} %constant.18.clone.back_ref) | copy-start | bytes 786436
  1.9 27.1 %copy-start.2 = (f32[40,256]{1,0:T(8,128)S(1)}, f32[40,256]{1,0:T(8,128)}, u32[]{:S(2)}) copy-start(f32[40,256]{1,0:T(8,128)} %constant.19.clone.turn_ref) | copy-start | bytes 122884

commit v9 on v7

--- a/solution.py
+++ b/solution.py
@@ -85,17 +85,15 @@
     own_sem,
 ):
     sections, length, channels = taps_ref.shape
-    mine_first = (
+    own_copies = (
         pltpu.make_async_copy(taps_ref, taps_held, own_sem.at[0]),
         pltpu.make_async_copy(gain_ref, gain_held, own_sem.at[1]),
     )
-    for copy in mine_first:
-        copy.start()
     arriving = (
         pltpu.make_async_copy(act_ref.at[0], act_held, in_sem.at[0]),
         pltpu.make_async_copy(filt_ref.at[0], filt_held, in_sem.at[1]),
     )
-    for copy in arriving:
+    for copy in (arriving[0], *own_copies, arriving[1]):
         copy.start()
     size = 128
     eye = identity(size)
@@ -105,12 +103,6 @@
     for position, rank in enumerate(order):
         place = place + jnp.where(place_ref[0] == rank, position, 0)
     pick = jnp.where((them == mine + place * owned) & (mine < owned), 1.0, 0.0)
-    for copy in mine_first:
-        copy.wait()
-    for s in range(sections):
-        gain = jnp.sum(pick * gain_held[s : s + 1, :], axis=1, keepdims=True)
-        own_ref[s * width : (s + 1) * width, :length] = dot_rows(pick.astype(jnp.bfloat16), taps_held[s])
-        own_ref[s * width : (s + 1) * width, length:] = jnp.broadcast_to(gain, (width, 128))
     def across(copy, held):
         copy.wait()
         columns = [
@@ -124,6 +116,12 @@
     for d in range(len(order) if even else 0):
         start = d * width
         out_ref[2 * start : 2 * start + even] = act[start : start + even].astype(jnp.bfloat16)
+    for copy in own_copies:
+        copy.wait()
+    for s in range(sections):
+        gain = jnp.sum(pick * gain_held[s : s + 1, :], axis=1, keepdims=True)
+        own_ref[s * width : (s + 1) * width, :length] = dot_rows(pick.astype(jnp.bfloat16), taps_held[s])
+        own_ref[s * width : (s + 1) * width, length:] = jnp.broadcast_to(gain, (width, 128))
     filt = across(arriving[1], filt_held)
     for d in range(len(order)):
         start, end = d * width, (d + 1) * width

time: 49.1 us -> 49.1 us (level)
  no operation moved by 1% of the time
where the time goes in v9:
time: 49.1 us; the launch traced here: 48.8 us
  blocking collectives  43.3 us (88%)
  Pallas kernels  5.46 us (11%)
    all_to_all x2, blocking collectives, exchanged(): lax.all_to_all(chunks, BOTH, split_axis=0, concat_axis=0, tiled=True, axi...  43.3 us
    pallas_call x1, Pallas kernels, body(): pl.pallas_call(functools.partial(main_kernel, width, sections, split, ord...  2.59 us
    pallas_call x1, Pallas kernels, body(): pl.pallas_call(functools.partial(send_kernel, width, owned, order), out_s...  1.82 us
    pallas_call x1, Pallas kernels, body(): pl.pallas_call(final_kernel, out_shape=jax.ShapeDtypeStruct((1, cols, lai...  1.05 us

profile of v9, /device:TPU:0, one launch (start us, length us, event | category | flops | bytes accessed | tf_op | source)
XLA Modules:
  0.0 48.8 jit_solution(18126509305765694723)
XLA Ops:
  0.0 1.8 %shard_map.73 = (bf16[1536,256]{1,0:T(8,128)(2,1)S(1)}, f32[48,256]{1,0:T(8,128)S(1)}) custom-call(s32[1]{0:T(128)} %bitcast.place_ref, bf16[1,256,768]{2,1,0:T(8,128)(2,1)} %act_ref.1, f32[1,256,768]{2,1,0:T(8,128)} %filt_ref.1, bf16[2,128,768]{2,1,0:T(8,128)(2,1)} %taps_ref.1, f32[2,768]{1,0:T(2,128)} %gain_ref.1), custom_call_target="tpu_custom_call" | custom-call | tf_op jit(solution)/shard_map/pallas_call | solution.py:295
  1.8 0.0 copy-start
  1.8 0.0 copy-start.1
  1.9 0.0 copy-start.2
  1.9 27.1 %all_to_all.10 = bf16[32,48,256]{2,1,0:T(8,128)(2,1)S(1)} all-to-all(bf16[32,48,256]{2,1,0:T(8,128)(2,1)S(1)} %bitcast.8), channel_id=1, replica_groups={{0,8,1,9,2,10,3,11,4,12,5,13,6,14,7,15,16,24,17,25,18,26,19,27,20,28,21..., dimensions={0} | all-to-all | bytes 1572864 | tf_op jit(solution)/shard_map/all_to_all | solution.py:275
  29.0 0.0 copy-done
  29.0 0.0 copy-done.1
  29.0 0.0 copy-done.2
  29.0 2.6 %shard_map.74 = bf16[768,256]{1,0:T(8,128)(2,1)S(1)} custom-call(bf16[1536,256]{1,0:T(8,128)(2,1)S(1)} %bitcast.5, f32[48,256]{1,0:T(8,128)S(1)} %get-tuple-element.8.own_ref, f32[40,256]{1,0:T(8,128)S(1)} %copy-done.2, bf16[784,256]{1,0:T(8,128)(2,1)S(1)} %copy-done, bf16[256,512]{1,0:T(8,128)(2,1)S(1)} %copy-done.1), custom_call_target="tpu_custom_call" | custom-call | tf_op jit(solution)/shard_map/pallas_call | solution.py:314
  31.6 16.2 %all_to_all.11 = bf16[32,24,256]{2,1,0:T(8,128)(2,1)S(1)} all-to-all(bf16[32,24,256]{2,1,0:T(8,128)(2,1)S(1)} %bitcast.7), channel_id=1, replica_groups={{0,8,1,9,2,10,3,11,4,12,5,13,6,14,7,15,16,24,17,25,18,26,19,27,20,28,21..., dimensions={0} | all-to-all | bytes 786432 | tf_op jit(solution)/shard_map/all_to_all | solution.py:275
  47.7 1.0 %shard_map.75 = bf16[1,256,768]{2,1,0:T(8,128)(2,1)} custom-call(bf16[768,256]{1,0:T(8,128)(2,1)S(1)} %bitcast.6), custom_call_target="tpu_custom_call" | custom-call | tf_op jit(solution)/shard_map/pallas_call | solution.py:322
Async XLA Ops:
  1.8 27.1 %copy-start = (bf16[784,256]{1,0:T(8,128)(2,1)S(1)}, bf16[784,256]{1,0:T(8,128)(2,1)}, u32[]{:S(2)}) copy-start(bf16[784,256]{1,0:T(8,128)(2,1)} %constant.17.clone.table_ref) | copy-start | bytes 1204228
  1.8 27.1 %copy-start.1 = (bf16[256,512]{1,0:T(8,128)(2,1)S(1)}, bf16[256,512]{1,0:T(8,128)(2,1)}, u32[]{:S(2)}) copy-start(bf16[256,512]{1,0:T(8,128)(2,1)} %constant.18.clone.back_ref) | copy-start | bytes 786436
  1.9 27.1 %copy-start.2 = (f32[40,256]{1,0:T(8,128)S(1)}, f32[40,256]{1,0:T(8,128)}, u32[]{:S(2)}) copy-start(f32[40,256]{1,0:T(8,128)} %constant.19.clone.turn_ref) | copy-start | bytes 122884

commit v10 on v7

--- a/solution.py
+++ b/solution.py
@@ -113,10 +113,13 @@
         own_ref[s * width : (s + 1) * width, length:] = jnp.broadcast_to(gain, (width, 128))
     def across(copy, held):
         copy.wait()
-        columns = [
-            dot_rows(eye, held[:, start : start + size].astype(jnp.bfloat16))
-            for start in range(0, held.shape[1], size)
-        ]
+        columns = []
+        for start in range(0, held.shape[1], size):
+            block = held[:, start : start + size]
+            if start // size % 2 and block.dtype == jnp.float32:
+                columns.append(block.T)
+            else:
+                columns.append(dot_rows(eye, block.astype(jnp.bfloat16)))
         return jnp.concatenate(columns, axis=0)
 
     even = width // 16 * 16

time: 49.1 us -> 49 us (level)
  no operation moved by 1% of the time
where the time goes in v10:
time: 49 us; the launch traced here: 48.7 us
  blocking collectives  43.3 us (88%)
  Pallas kernels  5.41 us (11%)
    all_to_all x2, blocking collectives, exchanged(): lax.all_to_all(chunks, BOTH, split_axis=0, concat_axis=0, tiled=True, axi...  43.3 us
    pallas_call x1, Pallas kernels, body(): pl.pallas_call(functools.partial(main_kernel, width, sections, split, ord...  2.59 us
    pallas_call x1, Pallas kernels, body(): pl.pallas_call(functools.partial(send_kernel, width, owned, order), out_s...  1.77 us
    pallas_call x1, Pallas kernels, body(): pl.pallas_call(final_kernel, out_shape=jax.ShapeDtypeStruct((1, cols, lai...  1.05 us

profile of v10, /device:TPU:0, one launch (start us, length us, event | category | flops | bytes accessed | tf_op | source)
XLA Modules:
  0.0 48.7 jit_solution(3980808358709912143)
XLA Ops:
  0.0 1.8 %shard_map.73 = (bf16[1536,256]{1,0:T(8,128)(2,1)S(1)}, f32[48,256]{1,0:T(8,128)S(1)}) custom-call(s32[1]{0:T(128)} %bitcast.place_ref, bf16[1,256,768]{2,1,0:T(8,128)(2,1)} %act_ref.1, f32[1,256,768]{2,1,0:T(8,128)} %filt_ref.1, bf16[2,128,768]{2,1,0:T(8,128)(2,1)} %taps_ref.1, f32[2,768]{1,0:T(2,128)} %gain_ref.1), custom_call_target="tpu_custom_call" | custom-call | tf_op jit(solution)/shard_map/pallas_call | solution.py:300
  1.8 0.0 copy-start
  1.8 0.0 copy-start.1
  1.8 0.0 copy-start.2
  1.8 27.1 %all_to_all.10 = bf16[32,48,256]{2,1,0:T(8,128)(2,1)S(1)} all-to-all(bf16[32,48,256]{2,1,0:T(8,128)(2,1)S(1)} %bitcast.8), channel_id=1, replica_groups={{0,8,1,9,2,10,3,11,4,12,5,13,6,14,7,15,16,24,17,25,18,26,19,27,20,28,21..., dimensions={0} | all-to-all | bytes 1572864 | tf_op jit(solution)/shard_map/all_to_all | solution.py:280
  28.9 0.0 copy-done
  28.9 0.0 copy-done.1
  28.9 0.0 copy-done.2
  28.9 2.6 %shard_map.74 = bf16[768,256]{1,0:T(8,128)(2,1)S(1)} custom-call(bf16[1536,256]{1,0:T(8,128)(2,1)S(1)} %bitcast.5, f32[48,256]{1,0:T(8,128)S(1)} %get-tuple-element.8.own_ref, f32[40,256]{1,0:T(8,128)S(1)} %copy-done.2, bf16[784,256]{1,0:T(8,128)(2,1)S(1)} %copy-done, bf16[256,512]{1,0:T(8,128)(2,1)S(1)} %copy-done.1), custom_call_target="tpu_custom_call" | custom-call | tf_op jit(solution)/shard_map/pallas_call | solution.py:319
  31.5 16.2 %all_to_all.11 = bf16[32,24,256]{2,1,0:T(8,128)(2,1)S(1)} all-to-all(bf16[32,24,256]{2,1,0:T(8,128)(2,1)S(1)} %bitcast.7), channel_id=1, replica_groups={{0,8,1,9,2,10,3,11,4,12,5,13,6,14,7,15,16,24,17,25,18,26,19,27,20,28,21..., dimensions={0} | all-to-all | bytes 786432 | tf_op jit(solution)/shard_map/all_to_all | solution.py:280
  47.7 1.0 %shard_map.75 = bf16[1,256,768]{2,1,0:T(8,128)(2,1)} custom-call(bf16[768,256]{1,0:T(8,128)(2,1)S(1)} %bitcast.6), custom_call_target="tpu_custom_call" | custom-call | tf_op jit(solution)/shard_map/pallas_call | solution.py:327
Async XLA Ops:
  1.8 27.1 %copy-start = (bf16[784,256]{1,0:T(8,128)(2,1)S(1)}, bf16[784,256]{1,0:T(8,128)(2,1)}, u32[]{:S(2)}) copy-start(bf16[784,256]{1,0:T(8,128)(2,1)} %constant.17.clone.table_ref) | copy-start | bytes 1204228
  1.8 27.1 %copy-start.1 = (bf16[256,512]{1,0:T(8,128)(2,1)S(1)}, bf16[256,512]{1,0:T(8,128)(2,1)}, u32[]{:S(2)}) copy-start(bf16[256,512]{1,0:T(8,128)(2,1)} %constant.18.clone.back_ref) | copy-start | bytes 786436
  1.8 27.1 %copy-start.2 = (f32[40,256]{1,0:T(8,128)S(1)}, f32[40,256]{1,0:T(8,128)}, u32[]{:S(2)}) copy-start(f32[40,256]{1,0:T(8,128)} %constant.19.clone.turn_ref) | copy-start | bytes 122884

commit v11 on v10

--- a/solution.py
+++ b/solution.py
@@ -135,13 +135,21 @@
         out_ref[2 * start + even : 2 * end] = rest.astype(jnp.bfloat16)
 
 
-def final_kernel(in_ref, out_ref):
+def final_kernel(in_ref, out_ref, held, sem):
     channels, tokens = in_ref.shape
     step = math.gcd(channels, 256)
+    half = tokens // 2
     eye = identity(tokens)
-    for start in range(0, channels, step):
-        part = slice(start, start + step)
-        out_ref[0, :, part] = dot_rows(eye, in_ref[part]).astype(jnp.bfloat16)
+    copies = []
+    for n in range(2):
+        rows = slice(n * half, (n + 1) * half)
+        for start in range(0, channels, step):
+            part = slice(start, start + step)
+            held[rows, part] = dot_rows(eye[rows], in_ref[part]).astype(jnp.bfloat16)
+        copies.append(pltpu.make_async_copy(held.at[rows], out_ref.at[0, rows], sem.at[n]))
+        copies[n].start()
+    for copy in copies:
+        copy.wait()
 
 
 def main_kernel(width, sections, split, order, in_ref, own_ref, turn_ref, table_ref, back_ref, out_ref):
@@ -327,6 +335,9 @@
     final = pl.pallas_call(
         final_kernel,
         out_shape=jax.ShapeDtypeStruct((1, cols, laid), jnp.bfloat16),
+        in_specs=[vmem],
+        out_specs=hbm,
+        scratch_shapes=[pltpu.VMEM((cols, laid), jnp.bfloat16), pltpu.SemaphoreType.DMA((2,))],
         compiler_params=grant(4 * MIB + 16 * area),
     )(returned)
     if width != owned:

time: 49 us -> 49.1 us (level)
  no operation moved by 1% of the time
where the time goes in v11:
time: 49.1 us; the launch traced here: 48.8 us
  blocking collectives  43.3 us (88%)
  Pallas kernels  5.45 us (11%)
    all_to_all x2, blocking collectives, exchanged(): lax.all_to_all(chunks, BOTH, split_axis=0, concat_axis=0, tiled=True, axi...  43.3 us
    pallas_call x1, Pallas kernels, body(): pl.pallas_call(functools.partial(main_kernel, width, sections, split, ord...  2.59 us
    pallas_call x1, Pallas kernels, body(): pl.pallas_call(functools.partial(send_kernel, width, owned, order), out_s...  1.77 us
    pallas_call x1, Pallas kernels, body(): pl.pallas_call(final_kernel, out_shape=jax.ShapeDtypeStruct((1, cols, lai...  1.09 us

profile of v11, /device:TPU:0, one launch (start us, length us, event | category | flops | bytes accessed | tf_op | source)
XLA Modules:
  0.0 48.8 jit_solution(17235506508723749773)
XLA Ops:
  0.0 1.8 %shard_map.73 = (bf16[1536,256]{1,0:T(8,128)(2,1)S(1)}, f32[48,256]{1,0:T(8,128)S(1)}) custom-call(s32[1]{0:T(128)} %bitcast.place_ref, bf16[1,256,768]{2,1,0:T(8,128)(2,1)} %act_ref.1, f32[1,256,768]{2,1,0:T(8,128)} %filt_ref.1, bf16[2,128,768]{2,1,0:T(8,128)(2,1)} %taps_ref.1, f32[2,768]{1,0:T(2,128)} %gain_ref.1), custom_call_target="tpu_custom_call" | custom-call | tf_op jit(solution)/shard_map/pallas_call | solution.py:308
  1.8 0.0 copy-start
  1.8 0.0 copy-start.1
  1.8 0.0 copy-start.2
  1.8 27.1 %all_to_all.10 = bf16[32,48,256]{2,1,0:T(8,128)(2,1)S(1)} all-to-all(bf16[32,48,256]{2,1,0:T(8,128)(2,1)S(1)} %bitcast.8), channel_id=1, replica_groups={{0,8,1,9,2,10,3,11,4,12,5,13,6,14,7,15,16,24,17,25,18,26,19,27,20,28,21..., dimensions={0} | all-to-all | bytes 1572864 | tf_op jit(solution)/shard_map/all_to_all | solution.py:288
  28.9 0.0 copy-done
  28.9 0.0 copy-done.1
  28.9 0.0 copy-done.2
  28.9 2.6 %shard_map.74 = bf16[768,256]{1,0:T(8,128)(2,1)S(1)} custom-call(bf16[1536,256]{1,0:T(8,128)(2,1)S(1)} %bitcast.5, f32[48,256]{1,0:T(8,128)S(1)} %get-tuple-element.8.own_ref, f32[40,256]{1,0:T(8,128)S(1)} %copy-done.2, bf16[784,256]{1,0:T(8,128)(2,1)S(1)} %copy-done, bf16[256,512]{1,0:T(8,128)(2,1)S(1)} %copy-done.1), custom_call_target="tpu_custom_call" | custom-call | tf_op jit(solution)/shard_map/pallas_call | solution.py:327
  31.5 16.2 %all_to_all.11 = bf16[32,24,256]{2,1,0:T(8,128)(2,1)S(1)} all-to-all(bf16[32,24,256]{2,1,0:T(8,128)(2,1)S(1)} %bitcast.7), channel_id=1, replica_groups={{0,8,1,9,2,10,3,11,4,12,5,13,6,14,7,15,16,24,17,25,18,26,19,27,20,28,21..., dimensions={0} | all-to-all | bytes 786432 | tf_op jit(solution)/shard_map/all_to_all | solution.py:288
  47.7 1.1 %shard_map.75 = bf16[1,256,768]{2,1,0:T(8,128)(2,1)} custom-call(bf16[768,256]{1,0:T(8,128)(2,1)S(1)} %bitcast.6), custom_call_target="tpu_custom_call" | custom-call | tf_op jit(solution)/shard_map/pallas_call | solution.py:335
Async XLA Ops:
  1.8 27.1 %copy-start = (bf16[784,256]{1,0:T(8,128)(2,1)S(1)}, bf16[784,256]{1,0:T(8,128)(2,1)}, u32[]{:S(2)}) copy-start(bf16[784,256]{1,0:T(8,128)(2,1)} %constant.17.clone.table_ref) | copy-start | bytes 1204228
  1.8 27.1 %copy-start.1 = (bf16[256,512]{1,0:T(8,128)(2,1)S(1)}, bf16[256,512]{1,0:T(8,128)(2,1)}, u32[]{:S(2)}) copy-start(bf16[256,512]{1,0:T(8,128)(2,1)} %constant.18.clone.back_ref) | copy-start | bytes 786436
  1.8 27.1 %copy-start.2 = (f32[40,256]{1,0:T(8,128)S(1)}, f32[40,256]{1,0:T(8,128)}, u32[]{:S(2)}) copy-start(f32[40,256]{1,0:T(8,128)} %constant.19.clone.turn_ref) | copy-start | bytes 122884

commit v12 on v10

--- a/solution.py
+++ b/solution.py
@@ -14,13 +14,20 @@
 MIB = 1024 * 1024
 
 
-def spread_order(devices, seq_devices):
-    half = seq_devices // 2
-    along = [place // 2 + place % 2 * half for place in range(2 * half)]
-    along += range(2 * half, seq_devices)
-    return tuple(
-        start + q for start in range(0, devices, seq_devices) for q in along
-    )
+FIELDS = {2: 7, 3: 11, 4: 19, 5: 37, 6: 67, 7: 131, 8: 285, 9: 529, 10: 1033}
+
+
+def spread_order(devices):
+    bits = devices.bit_length() - 1
+    if devices != 1 << bits or bits not in FIELDS:
+        return tuple(range(devices))
+    order, power = [0], 1
+    while len(order) < devices:
+        order.append(power)
+        power <<= 1
+        if power & devices:
+            power ^= FIELDS[bits]
+    return tuple(order)
 
 
 def tables(real_rows, cols, split):
@@ -268,7 +275,7 @@
     width = -(-owned // LANES) * LANES
     cols = tokens
     laid = devices * width
-    order = spread_order(devices, seq_devices)
+    order = spread_order(devices)
 
     def widen(array):
         split = array.reshape(array.shape[:2] + (devices, owned))

time: 49 us -> 49.2 us (level)
  no operation moved by 1% of the time
where the time goes in v12:
time: 49.2 us; the launch traced here: 49 us
  blocking collectives  43.6 us (89%)
  Pallas kernels  5.39 us (11%)
    all_to_all x2, blocking collectives, exchanged(): lax.all_to_all(chunks, BOTH, split_axis=0, concat_axis=0, tiled=True, axi...  43.6 us
    pallas_call x1, Pallas kernels, body(): pl.pallas_call(functools.partial(main_kernel, width, sections, split, ord...  2.58 us
    pallas_call x1, Pallas kernels, body(): pl.pallas_call(functools.partial(send_kernel, width, owned, order), out_s...  1.77 us
    pallas_call x1, Pallas kernels, body(): pl.pallas_call(final_kernel, out_shape=jax.ShapeDtypeStruct((1, cols, lai...  1.05 us

profile of v12, /device:TPU:0, one launch (start us, length us, event | category | flops | bytes accessed | tf_op | source)
XLA Modules:
  0.0 49.0 jit_solution(7717608673243236981)
XLA Ops:
  0.0 1.8 %shard_map.73 = (bf16[1536,256]{1,0:T(8,128)(2,1)S(1)}, f32[48,256]{1,0:T(8,128)S(1)}) custom-call(s32[1]{0:T(128)} %bitcast.place_ref, bf16[1,256,768]{2,1,0:T(8,128)(2,1)} %act_ref.1, f32[1,256,768]{2,1,0:T(8,128)} %filt_ref.1, bf16[2,128,768]{2,1,0:T(8,128)(2,1)} %taps_ref.1, f32[2,768]{1,0:T(2,128)} %gain_ref.1), custom_call_target="tpu_custom_call" | custom-call | tf_op jit(solution)/shard_map/pallas_call | solution.py:307
  1.8 0.0 copy-start
  1.8 0.0 copy-start.1
  1.8 0.0 copy-start.2
  1.8 26.1 %all_to_all.10 = bf16[32,48,256]{2,1,0:T(8,128)(2,1)S(1)} all-to-all(bf16[32,48,256]{2,1,0:T(8,128)(2,1)S(1)} %bitcast.8), channel_id=1, replica_groups={{0,1,2,4,8,16,5,10,20,13,26,17,7,14,28,29,31,27,19,3,6,12,24,21,15,30,2..., dimensions={0} | all-to-all | bytes 1572864 | tf_op jit(solution)/shard_map/all_to_all | solution.py:287
  27.9 0.0 copy-done
  27.9 0.0 copy-done.1
  27.9 0.0 copy-done.2
  27.9 2.6 %shard_map.74 = bf16[768,256]{1,0:T(8,128)(2,1)S(1)} custom-call(bf16[1536,256]{1,0:T(8,128)(2,1)S(1)} %bitcast.5, f32[48,256]{1,0:T(8,128)S(1)} %get-tuple-element.8.own_ref, f32[40,256]{1,0:T(8,128)S(1)} %copy-done.2, bf16[784,256]{1,0:T(8,128)(2,1)S(1)} %copy-done, bf16[256,512]{1,0:T(8,128)(2,1)S(1)} %copy-done.1), custom_call_target="tpu_custom_call" | custom-call | tf_op jit(solution)/shard_map/pallas_call | solution.py:326
  30.5 17.5 %all_to_all.11 = bf16[32,24,256]{2,1,0:T(8,128)(2,1)S(1)} all-to-all(bf16[32,24,256]{2,1,0:T(8,128)(2,1)S(1)} %bitcast.7), channel_id=1, replica_groups={{0,1,2,4,8,16,5,10,20,13,26,17,7,14,28,29,31,27,19,3,6,12,24,21,15,30,2..., dimensions={0} | all-to-all | bytes 786432 | tf_op jit(solution)/shard_map/all_to_all | solution.py:287
  48.0 1.0 %shard_map.75 = bf16[1,256,768]{2,1,0:T(8,128)(2,1)} custom-call(bf16[768,256]{1,0:T(8,128)(2,1)S(1)} %bitcast.6), custom_call_target="tpu_custom_call" | custom-call | tf_op jit(solution)/shard_map/pallas_call | solution.py:334
Async XLA Ops:
  1.8 26.1 %copy-start = (bf16[784,256]{1,0:T(8,128)(2,1)S(1)}, bf16[784,256]{1,0:T(8,128)(2,1)}, u32[]{:S(2)}) copy-start(bf16[784,256]{1,0:T(8,128)(2,1)} %constant.17.clone.table_ref) | copy-start | bytes 1204228
  1.8 26.1 %copy-start.1 = (bf16[256,512]{1,0:T(8,128)(2,1)S(1)}, bf16[256,512]{1,0:T(8,128)(2,1)}, u32[]{:S(2)}) copy-start(bf16[256,512]{1,0:T(8,128)(2,1)} %constant.18.clone.back_ref) | copy-start | bytes 786436
  1.8 26.1 %copy-start.2 = (f32[40,256]{1,0:T(8,128)S(1)}, f32[40,256]{1,0:T(8,128)}, u32[]{:S(2)}) copy-start(f32[40,256]{1,0:T(8,128)} %constant.19.clone.turn_ref) | copy-start | bytes 122884
